TPU v7x, 512 devices: a whole 4x4x16 slice. The times are simulated.
512 devices in a mesh: lon: 64 (over y, z_hi, x, core), tm: 8 (over z_lo).
Axes of the slice: x: 4, y: 4, z: 16 (z_hi: 2, z_lo: 8; z = z_hi * 8 + z_lo), core: 2. Of those that a mesh axis runs over, the one named last changes fastest.
Arguments:
- queries: bfloat16 [8, 256, 32, 1024], P('tm', 'lon'), may hold values from -8 to 8
- token_keys: bfloat16 [8, 256, 32, 1024], P('tm', 'lon'), may hold values from -8 to 8
- values: bfloat16 [8, 256, 32, 1024], P('tm', 'lon'), may hold values from -6 to 6
- grad_out: bfloat16 [8, 256, 32, 1024], P('tm', 'lon'), may hold values from -6 to 6
- window_shifts: int32 [8, 2], replicated, may hold values from 0 to 7
- noise_steps: int32 [8], replicated, may hold values from 0 to 63
- gate_table: float32 [64, 1024], replicated, may hold values from -4 to 4
Outputs:
- d_queries: bfloat16 [8, 256, 32, 1024], P('tm', 'lon')
- d_keys: bfloat16 [8, 256, 32, 1024], P('tm', 'lon')
- d_values: bfloat16 [8, 256, 32, 1024], P('tm', 'lon')
All inputs are finite; a program needn't handle non-finite values.
Results may differ from a plain program's by a relative error of at most 0.0073.
Values may be sent and summed in bfloat16 or wider, within the bound.
No kernel may reach another device: no remote copies, remote signals or barrier semaphores. Data moves between devices by JAX's collectives and lax.ppermute only.
A program may use at most 64 MiB of HBM per device.

v0:
```python
import jax
import jax.numpy as jnp
from jax import lax
from jax.experimental import pallas as pl
from jax.experimental.pallas import tpu as pltpu
from jax.sharding import PartitionSpec as P

HEAD_DIM = 64
WIN = 8
LANES = 128
PAIRS = 4
SLOTS = 9
HALF = 5
ROW = 4
SCALE = HEAD_DIM**-0.5
NEG = -1e30
VMEM = pl.BlockSpec(memory_space=pltpu.VMEM)
SMEM = pl.BlockSpec(memory_space=pltpu.SMEM)
ANY = pl.BlockSpec(memory_space=pl.ANY)
SPATIAL_FLOPS = 480 << 26
TEMPORAL_FLOPS = 1 << 20
GATHER_FLOPS = 84 << 28
BF16 = jnp.bfloat16
F32 = jnp.float32


def low_pairs(b):
    one = jnp.int32(1)
    zero = jnp.int32(0)
    return sum(jnp.where(b < top, one, zero) for top in (2, 4, 5, 7))


def call(body, outs, in_specs, flops, nbytes, scratch=(), mib=48):
    return pl.pallas_call(
        body,
        out_shape=[jax.ShapeDtypeStruct(s, BF16) for s in outs],
        in_specs=in_specs,
        out_specs=[VMEM] * len(outs),
        scratch_shapes=list(scratch),
        compiler_params=pltpu.CompilerParams(vmem_limit_bytes=mib << 20),
        cost_estimate=pl.CostEstimate(flops=flops, bytes_accessed=nbytes, transcendentals=0),
    )


def split_body(scal, q, k, v, g, stacked, own, other, held, sems):
    core = scal[2]
    copies = [pltpu.make_async_copy(ref, held.at[r], sems.at[r]) for r, ref in enumerate((q, k, v, g))]
    for copy in copies:
        copy.start()
    for r, copy in enumerate(copies):
        copy.wait()
        for i in range(8):
            stacked[i, 16 * r : 16 * r + 16, :] = held[r, 16 * i : 16 * i + 16, :]
        for half in range(2):

            @pl.when(core == half)
            def _(r=r, half=half):
                for p in range(PAIRS):
                    lo = half * PAIRS * LANES + p * LANES
                    hi = (1 - half) * PAIRS * LANES + p * LANES
                    own[r, p] = held[r, :, lo : lo + LANES].reshape(4, 32, LANES)
                    other[r, p] = held[r, :, hi : hi + LANES].reshape(4, 32, LANES)


def row_end(scal):
    return scal[3] == 0, scal[3] == 3


def store_block(slot, count, block, side, cross_a, cross_b, crosses):
    for r in range(count):
        side[r, slot] = block(r)

    @pl.when(jnp.logical_and(crosses, slot < HALF))
    def _():
        for r in range(count):
            cross_a[r, slot] = block(r)

    @pl.when(jnp.logical_and(crosses, slot >= HALF))
    def _():
        for r in range(count):
            cross_b[r, slot - HALF] = block(r)


def load_block(slot, count, put, side, cross_a, cross_b, crosses):
    @pl.when(jnp.logical_not(crosses))
    def _():
        for r in range(count):
            put(r, side[r, slot])

    @pl.when(jnp.logical_and(crosses, slot < HALF))
    def _():
        for r in range(count):
            put(r, cross_a[r, slot])

    @pl.when(jnp.logical_and(crosses, slot >= HALF))
    def _():
        for r in range(count):
            put(r, cross_b[r, slot - HALF])


def halo_body(scal, own, got, whole, to_left, to_right, cross_a, cross_b):
    b = scal[1]
    core = scal[2]
    first, last = row_end(scal)
    n_low = low_pairs(b)
    for r in range(4):
        for p in range(PAIRS):
            whole[r, p, pl.ds(core * 4, 4)] = own[r, p]
            whole[r, p, pl.ds((1 - core) * 4, 4)] = got[r, p]
    for p in range(PAIRS):

        @pl.when(p < n_low)
        def _(p=p):
            def put(col, carry):
                block = lambda r: whole[r, p, col]
                store_block(p * b + col, 4, block, to_left, cross_a, cross_b, first)
                return carry

            lax.fori_loop(0, b, put, 0)

        @pl.when(p >= n_low)
        def _(p=p):
            def put(col, carry):
                block = lambda r: whole[r, p, col]
                slot = (p - n_low) * (8 - b) + col - b
                store_block(slot, 4, block, to_right, cross_a, cross_b, last)
                return carry

            lax.fori_loop(b, 8, put, 0)


def attend(q, k, v, g, mask):
    tokens = q.shape[0]
    lane = lax.broadcasted_iota(jnp.int32, (1, LANES), 1)
    first = jnp.where(lane < HEAD_DIM, 1.0, 0.0).astype(BF16)
    second = jnp.where(lane < HEAD_DIM, 0.0, 1.0).astype(BF16)
    q = q * jnp.asarray(SCALE, BF16)
    q2 = jnp.concatenate([q * first, q * second], axis=0)
    g2 = jnp.concatenate([g * first, g * second], axis=0)
    over_last = (((1,), (1,)), ((), ()))
    over_first = (((0,), (0,)), ((), ()))
    s = lax.dot_general(q2, k, over_last, preferred_element_type=F32)
    dp = lax.dot_general(g2, v, over_last, preferred_element_type=F32)
    s = jnp.where(mask, s, NEG)
    e = jnp.exp(s - jnp.max(s, axis=1, keepdims=True))
    p = e * (1.0 / jnp.sum(e, axis=1, keepdims=True))
    delta = jnp.sum(p * dp, axis=1, keepdims=True)
    ds = (p * (dp - delta)).astype(BF16)
    p = p.astype(BF16)
    dv = lax.dot_general(p, g2, over_first, preferred_element_type=F32)
    dk = lax.dot_general(ds, q2, over_first, preferred_element_type=F32)
    dq = jnp.dot(ds[:tokens], k * first, preferred_element_type=F32)
    dq = dq + jnp.dot(ds[tokens:], k * second, preferred_element_type=F32)
    return (dq * SCALE, dk, dv)


def spatial_body(
    scal, whole, from_left, from_right, in_a, in_b,
    local, back_left, back_right, out_a, out_b, strip, grads,
):
    a = scal[0]
    b = scal[1]
    first, last = row_end(scal)
    n_low = low_pairs(b)
    tokens = 8 * 32

    def block_of(dim, shape):
        row = lax.broadcasted_iota(jnp.int32, shape, dim) & 31
        return (row + WIN - a) >> 3

    mask = block_of(0, (2 * tokens, tokens)) == block_of(1, (2 * tokens, tokens))

    def per_pair(p, carry):
        low = p < n_low

        def place(col):
            here = jnp.logical_xor(low, col < b)
            there = jnp.logical_not(here)
            on_right = jnp.logical_and(there, low)
            on_left = jnp.logical_and(there, jnp.logical_not(low))
            return here, on_left, on_right, p * b + col, (p - n_low) * (8 - b) + col - b

        def fetch(col, inner):
            here, on_left, on_right, slot_right, slot_left = place(col)

            def put(r, block):
                strip[r, col] = block

            @pl.when(here)
            def _():
                for r in range(4):
                    strip[r, col] = whole[r, p, col]

            @pl.when(on_right)
            def _():
                load_block(slot_right, 4, put, from_right, in_a, in_b, last)

            @pl.when(on_left)
            def _():
                load_block(slot_left, 4, put, from_left, in_a, in_b, first)

            return inner

        lax.fori_loop(0, 8, fetch, 0)
        q, k, v, g = (strip[r].reshape(tokens, LANES) for r in range(4))
        for r, grad in enumerate(attend(q, k, v, g, mask)):
            grads[r] = grad.astype(BF16).reshape(8, 32, LANES)

        def store(col, inner):
            here, on_left, on_right, slot_right, slot_left = place(col)
            block = lambda r: grads[r, col]

            @pl.when(here)
            def _():
                for r in range(3):
                    local[r, p, col] = grads[r, col]

            @pl.when(on_right)
            def _():
                store_block(slot_right, 3, block, back_right, out_a, out_b, last)

            @pl.when(on_left)
            def _():
                store_block(slot_left, 3, block, back_left, out_a, out_b, first)

            return inner

        lax.fori_loop(0, 8, store, 0)
        return carry

    lax.fori_loop(0, PAIRS, per_pair, 0)


def gather_body(scal, local, from_left, from_right, in_a, in_b, keep, send):
    b = scal[1]
    core = scal[2]
    first, last = row_end(scal)
    n_low = low_pairs(b)
    for p in range(PAIRS):
        low = p < n_low

        def move(col, target, p=p, low=low):
            here = jnp.logical_xor(low, col < b)
            there = jnp.logical_not(here)
            spot = col & 3

            def put(r, block):
                target[r, p, spot] = block

            @pl.when(here)
            def _():
                for r in range(3):
                    target[r, p, spot] = local[r, p, col]

            @pl.when(jnp.logical_and(there, low))
            def _():
                load_block(p * b + col, 3, put, from_left, in_a, in_b, first)

            @pl.when(jnp.logical_and(there, jnp.logical_not(low)))
            def _():
                slot = (p - n_low) * (8 - b) + col - b
                load_block(slot, 3, put, from_right, in_a, in_b, last)

        for i in range(4):
            move(core * 4 + i, keep)
            move((1 - core) * 4 + i, send)


def temporal_body(steps, arrived, table, out, gates):
    frames = 8
    tokens = frames * 16
    for f in range(frames):
        gates[f] = table[pl.ds(steps[f], 1), :]

    def spot(dim, shape):
        return lax.broadcasted_iota(jnp.int32, shape, dim) & 15

    mask = spot(0, (2 * tokens, tokens)) == spot(1, (2 * tokens, tokens))
    for p in range(8):
        lanes = slice(p * LANES, (p + 1) * LANES)
        q, k, v, g = (arrived[:, 16 * r : 16 * r + 16, lanes] for r in range(4))
        g = (g.astype(F32) * gates[:, :, lanes]).astype(BF16)
        q, k, v, g = (x.reshape(tokens, LANES) for x in (q, k, v, g))
        for r, grad in enumerate(attend(q, k, v, g, mask)):
            out[:, 16 * r : 16 * r + 16, lanes] = grad.astype(BF16).reshape(frames, 16, LANES)


def final_body(scal, keep, got, times, dq, dk, dv):
    core = scal[2]
    for half in range(2):

        @pl.when(core == half)
        def _():
            for r, out in enumerate((dq, dk, dv)):
                for side, part in ((half, keep), (1 - half, got)):
                    for p in range(PAIRS):
                        lo = side * PAIRS * LANES + p * LANES
                        space = part[r, p].astype(F32).reshape(8, 16, LANES)
                        time = times[:, 16 * r : 16 * r + 16, lo : lo + LANES].astype(F32)
                        out[:, lo : lo + LANES] = (space + time).astype(BF16).reshape(128, LANES)


def exchange(to_left, to_right, cross_a, cross_b):
    devices = lax.axis_size("lon")
    chips = devices // 2

    def moves(by):
        return [
            (i, ((i // 2 + by[i // 2 % ROW]) % chips) * 2 + i % 2)
            for i in range(devices)
            if i // 2 % ROW in by
        ]

    def send(x, by):
        return lax.ppermute(x, "lon", moves(by))

    beside = send(cross_b, {3: -1, 0: 1})
    from_left = send(to_right, {0: 1, 1: 1, 2: 1})
    from_right = send(to_left, {1: -1, 2: -1, 3: -1})
    column = (lax.axis_index("lon") >> 1) & 3
    outer = jnp.logical_or(column == 0, column == 3)
    far = send(jnp.where(outer, cross_a, beside), {3: ROW, 2: ROW, 1: -ROW, 0: -ROW})
    in_a = send(far, {3: -3, 0: 3})
    in_b = send(far, {2: -2, 1: 2})
    return beside, (from_left, from_right, in_a, in_b)


def shards(queries, token_keys, values, grad_out, window_shifts, noise_steps, gate_table):
    devices = lax.axis_size("lon")

    def core_swap(x):
        return lax.ppermute(x, "lon", [(i, i ^ 1) for i in range(devices)])

    def over_frames(x):
        return lax.all_to_all(x, "tm", split_axis=0, concat_axis=0, tiled=True)

    frame = lax.axis_index("tm")
    lon = lax.axis_index("lon")
    shift = lax.dynamic_slice_in_dim(window_shifts, frame, 1, 0).reshape(2)
    place = jnp.stack([lon & 1, (lon >> 1) & 3]).astype(jnp.int32)
    scal = jnp.concatenate([shift, place])
    flat = [x.reshape(128, 1024) for x in (queries, token_keys, values, grad_out)]
    half = (4, PAIRS, 4, 32, LANES)

    def sides(count):
        side = (count, SLOTS, 32, LANES)
        return [side, side, (count, HALF, 32, LANES), (count, HALF, 32, LANES)]

    with jax.named_scope("split"):
        stacked, own, other = call(
            split_body, [(8, 64, 1024), half, half], [SMEM] + [ANY] * 4, 1 << 20, 3 << 20,
            [pltpu.VMEM((4, 128, 1024), BF16), pltpu.SemaphoreType.DMA((4,))], 60,
        )(scal, *flat)
    got = core_swap(other)
    with jax.named_scope("halo"):
        whole, *out = call(
            halo_body, [(4, PAIRS, 8, 32, LANES)] + sides(4), [SMEM] + [VMEM] * 2, 1 << 20, 3 << 20
        )(scal, own, got)
    beside, arriving = exchange(*out)
    stacked, _ = lax.optimization_barrier((stacked, beside))
    arrived = over_frames(stacked)
    with jax.named_scope("spatial"):
        local, *back = call(
            spatial_body, [(3, PAIRS, 8, 32, LANES)] + sides(3), [SMEM] + [VMEM] * 5, SPATIAL_FLOPS, 4 << 20,
            [pltpu.VMEM((4, 8, 32, LANES), BF16), pltpu.VMEM((3, 8, 32, LANES), BF16)],
        )(scal, whole, *arriving)
    beside, returned = exchange(*back)
    arrived, _ = lax.optimization_barrier((arrived, beside))
    with jax.named_scope("temporal"):
        (out_time,) = call(
            temporal_body, [(8, 48, 1024)], [SMEM, VMEM, VMEM], TEMPORAL_FLOPS, 4 << 20,
            [pltpu.VMEM((8, 1, 1024), F32)],
        )(noise_steps, arrived, gate_table)
    times = over_frames(out_time)
    with jax.named_scope("gather"):
        keep, send = call(
            gather_body, [(3, PAIRS, 4, 32, LANES)] * 2, [SMEM] + [VMEM] * 5, GATHER_FLOPS, 2 << 20
        )(scal, local, *returned)
    got_back = core_swap(send)
    with jax.named_scope("final"):
        outs = call(final_body, [(128, 1024)] * 3, [SMEM] + [VMEM] * 3, 1 << 20, 3 << 20)(
            scal, keep, got_back, times
        )
    return tuple(x.reshape(1, 4, 32, 1024) for x in outs)


def solution(mesh):
    placed = P("tm", "lon", None, None)
    return jax.shard_map(
        shards,
        mesh=mesh,
        in_specs=(placed, placed, placed, placed, P(), P(), P()),
        out_specs=(placed, placed, placed),
        check_vma=False,
    )
```

profile of v0, /device:TPU:2, one launch (start us, length us, event | category | flops | bytes accessed | tf_op | source)
XLA Modules:
  0.0 162.7 jit_solution(17349865721554386461)
XLA Ops:
  0.6 0.0 copy-start
  0.7 0.7 copy-done
  1.3 0.2 dynamic-slice_reduce_fusion
  1.5 0.6 pad_add_fusion.scal
  2.1 3.3 %split.1 = (bf16[8,64,1024]{2,1,0:T(8,128)(2,1)}, bf16[4,4,4,32,128]{4,3,2,1,0:T(8,128)(2,1)}, bf16[4,4,4,32,128]{4,3,2,1,0:T(8,128)(2,1)}) custom-call(s32[4]{0:T(128)} %pad_add_fusion.scal, bf16[128,1024]{1,0:T(8,128)(2,1)} %bitcast.9, bf16[128,1024]{1,0:T(8,128)(2,1)} %bitcast.10, bf16[128,1024]{1,0:T(8,128)(2,1)} %bitcast.11, bf16[128,1024]{1,0:T(8,128)(2,1)} %bitcast.12), custom_call_target="tpu_custom_call" | custom-call | flops 1048576 | bytes 3145728 | tf_op jit(solution)/shard_map/split/pallas_call | solution.py:350
  5.4 0.0 copy-start.3
  5.4 1.9 %collective-permute-start = (bf16[4,4,4,32,128]{4,3,2,1,0:T(8,128)(2,1)}, bf16[4,4,4,32,128]{4,3,2,1,0:T(8,128)(2,1)S(1)}, u32[]{:S(2)}, u32[]{:S(2)}) collective-permute-start(bf16[4,4,4,32,128]{4,3,2,1,0:T(8,128)(2,1)} %get-tuple-element.24), channel_id=1, source_target_pairs={{0,8},{8,0},{16,24},{24,16},{32,40},{40,32},{48,56},{56,48},{64,72... | collective-permute-start | bytes 1572872 | tf_op jit(solution)/shard_map/ppermute | solution.py:332
  7.3 2.1 %collective-permute-done.got = bf16[4,4,4,32,128]{4,3,2,1,0:T(8,128)(2,1)S(1)} collective-permute-done((bf16[4,4,4,32,128]{4,3,2,1,0:T(8,128)(2,1)}, bf16[4,4,4,32,128]{4,3,2,1,0:T(8,128)(2,1)S(1)}, u32[]{:S(2)}, u32[]{:S(2)}) %collective-permute-start) | collective-permute-done | bytes 524320 | tf_op jit(solution)/shard_map/ppermute | solution.py:332
  9.4 0.0 copy-done.3
  9.4 0.0 copy-start.1
  9.4 1.0 copy-done.1
  10.4 0.7 halo.1
  11.1 1.3 collective-permute-start.3
  12.4 10.4 %collective-permute-done.3 = bf16[4,5,32,128]{3,2,1,0:T(8,128)(2,1)S(1)} collective-permute-done((bf16[4,5,32,128]{3,2,1,0:T(8,128)(2,1)S(1)}, bf16[4,5,32,128]{3,2,1,0:T(8,128)(2,1)S(1)}, u32[]{:S(2)}, u32[]{:S(2)}) %collective-permute-start.3) | collective-permute-done | bytes 163872 | tf_op jit(solution)/shard_map/ppermute | solution.py:315
  22.8 14.6 %collective-permute-start.4 = (bf16[4,5,32,128]{3,2,1,0:T(8,128)(2,1)S(1)}, bf16[4,5,32,128]{3,2,1,0:T(8,128)(2,1)}, u32[]{:S(2)}, u32[]{:S(2)}) collective-permute-start(bf16[4,5,32,128]{3,2,1,0:T(8,128)(2,1)S(1)} %broadcast_select_fusion), channel_id=1, source_target_pairs={{0,448},{8,456},{16,464},{24,472},{32,96},{40,104},{48,112},{56,12... | collective-permute-start | bytes 491528 | tf_op jit(solution)/shard_map/ppermute | solution.py:315
  37.5 1.9 %collective-permute-start.1 = (bf16[4,9,32,128]{3,2,1,0:T(8,128)(2,1)S(1)}, bf16[4,9,32,128]{3,2,1,0:T(8,128)(2,1)S(1)}, u32[]{:S(2)}, u32[]{:S(2)}) collective-permute-start(bf16[4,9,32,128]{3,2,1,0:T(8,128)(2,1)S(1)} %get-tuple-element.26), channel_id=1, source_target_pairs={{0,16},{8,24},{16,32},{24,40},{32,48},{40,56},{64,80},{72,88},{80,... | collective-permute-start | bytes 884744 | tf_op jit(solution)/shard_map/ppermute | solution.py:315
  39.4 3.9 %collective-permute-start.2 = (bf16[4,9,32,128]{3,2,1,0:T(8,128)(2,1)S(1)}, bf16[4,9,32,128]{3,2,1,0:T(8,128)(2,1)S(1)}, u32[]{:S(2)}, u32[]{:S(2)}) collective-permute-start(bf16[4,9,32,128]{3,2,1,0:T(8,128)(2,1)S(1)} %get-tuple-element.27), channel_id=1, source_target_pairs={{16,0},{24,8},{32,16},{40,24},{48,32},{56,40},{80,64},{88,72},{96,... | collective-permute-start | bytes 884744 | tf_op jit(solution)/shard_map/ppermute | solution.py:315
  43.3 5.2 %all-to-all-start = ((bf16[8,64,1024]{2,1,0:T(8,128)(2,1)}), bf16[8,64,1024]{2,1,0:T(8,128)(2,1)S(1)}, u32[]{:S(2)}, u32[]{:S(2)}) async-start(bf16[8,64,1024]{2,1,0:T(8,128)(2,1)} %get-tuple-element.38), calls=%async_computation | async-start | bytes 2097152 | tf_op jit(solution)/shard_map/all_to_all | solution.py:335
  48.6 1.7 %collective-permute-done.4 = bf16[4,5,32,128]{3,2,1,0:T(8,128)(2,1)} collective-permute-done((bf16[4,5,32,128]{3,2,1,0:T(8,128)(2,1)S(1)}, bf16[4,5,32,128]{3,2,1,0:T(8,128)(2,1)}, u32[]{:S(2)}, u32[]{:S(2)}) %collective-permute-start.4) | collective-permute-done | bytes 163872 | tf_op jit(solution)/shard_map/ppermute | solution.py:315
  50.3 1.3 collective-permute-start.6
  51.6 0.7 collective-permute-start.5
  52.3 0.0 collective-permute-done.1.from_left
  52.3 0.0 collective-permute-done.2.from_right
  52.3 2.5 %collective-permute-done.6.in_b = bf16[4,5,32,128]{3,2,1,0:T(8,128)(2,1)S(1)} collective-permute-done((bf16[4,5,32,128]{3,2,1,0:T(8,128)(2,1)}, bf16[4,5,32,128]{3,2,1,0:T(8,128)(2,1)S(1)}, u32[]{:S(2)}, u32[]{:S(2)}) %collective-permute-start.6) | collective-permute-done | bytes 163872 | tf_op jit(solution)/shard_map/ppermute | solution.py:315
  54.8 0.0 collective-permute-done.5.in_a
  54.8 6.1 %spatial.1 = (bf16[3,4,8,32,128]{4,3,2,1,0:T(8,128)(2,1)S(1)}, bf16[3,9,32,128]{3,2,1,0:T(8,128)(2,1)S(1)}, bf16[3,9,32,128]{3,2,1,0:T(8,128)(2,1)S(1)}, bf16[3,...) custom-call(s32[4]{0:T(128)S(1)} %copy-done.3, bf16[4,4,8,32,128]{4,3,2,1,0:T(8,128)(2,1)S(1)} %get-tuple-element.25.whole, ...), custom_call_target="tpu_custom_call" | custom-call | flops 32212254720 | bytes 4194304 | tf_op jit(solution)/shard_map/spatial/pallas_call | solution.py:363
  60.9 0.0 copy-start.5
  60.9 0.9 copy-done.5
  61.8 0.0 copy-start.2
  61.8 1.4 collective-permute-start.9
  63.2 8.4 %collective-permute-done.9 = bf16[3,5,32,128]{3,2,1,0:T(8,128)(2,1)S(1)} collective-permute-done((bf16[3,5,32,128]{3,2,1,0:T(8,128)(2,1)S(1)}, bf16[3,5,32,128]{3,2,1,0:T(8,128)(2,1)S(1)}, u32[]{:S(2)}, u32[]{:S(2)}) %collective-permute-start.9) | collective-permute-done | bytes 122912 | tf_op jit(solution)/shard_map/ppermute | solution.py:315
  71.6 0.0 copy-start.4
  71.6 15.7 %collective-permute-start.10 = (bf16[3,5,32,128]{3,2,1,0:T(8,128)(2,1)S(1)}, bf16[3,5,32,128]{3,2,1,0:T(8,128)(2,1)S(1)}, u32[]{:S(2)}, u32[]{:S(2)}) collective-permute-start(bf16[3,5,32,128]{3,2,1,0:T(8,128)(2,1)S(1)} %broadcast_select_fusion.1), channel_id=1, source_target_pairs={{0,448},{8,456},{16,464},{24,472},{32,96},{40,104},{48,112},{56,12... | collective-permute-start | bytes 368648 | tf_op jit(solution)/shard_map/ppermute | solution.py:315
  87.3 21.7 %all-to-all-done.arrived = bf16[8,64,1024]{2,1,0:T(8,128)(2,1)S(1)} async-done(((bf16[8,64,1024]{2,1,0:T(8,128)(2,1)}), bf16[8,64,1024]{2,1,0:T(8,128)(2,1)S(1)}, u32[]{:S(2)}, u32[]{:S(2)}) %all-to-all-start) | async-done | bytes 1048608 | tf_op jit(solution)/shard_map/all_to_all | solution.py:335
  109.0 0.0 copy-done.2
  109.0 0.0 copy-done.4
  109.0 5.4 %temporal.1 = bf16[8,48,1024]{2,1,0:T(8,128)(2,1)} custom-call(s32[8]{0:T(128)S(1)} %copy-done.4, bf16[8,64,1024]{2,1,0:T(8,128)(2,1)S(1)} %all-to-all-done.arrived, f32[64,1024]{1,0:T(8,128)S(1)} %copy-done.2), custom_call_target="tpu_custom_call" | custom-call | flops 1048576 | bytes 4194304 | tf_op jit(solution)/shard_map/temporal/pallas_call | solution.py:370
  114.4 0.0 copy-start.6
  114.4 6.4 %all-to-all-start.1 = ((bf16[8,48,1024]{2,1,0:T(8,128)(2,1)}), bf16[8,48,1024]{2,1,0:T(8,128)(2,1)S(1)}, u32[]{:S(2)}, u32[]{:S(2)}) async-start(bf16[8,48,1024]{2,1,0:T(8,128)(2,1)} %temporal.1), calls=%async_computation.1 | async-start | bytes 1572864 | tf_op jit(solution)/shard_map/all_to_all | solution.py:335
  120.9 1.9 %collective-permute-start.7 = (bf16[3,9,32,128]{3,2,1,0:T(8,128)(2,1)S(1)}, bf16[3,9,32,128]{3,2,1,0:T(8,128)(2,1)S(1)}, u32[]{:S(2)}, u32[]{:S(2)}) collective-permute-start(bf16[3,9,32,128]{3,2,1,0:T(8,128)(2,1)S(1)} %get-tuple-element.31), channel_id=1, source_target_pairs={{0,16},{8,24},{16,32},{24,40},{32,48},{40,56},{64,80},{72,88},{80,... | collective-permute-start | bytes 663560 | tf_op jit(solution)/shard_map/ppermute | solution.py:315
  122.8 3.9 %collective-permute-start.8 = (bf16[3,9,32,128]{3,2,1,0:T(8,128)(2,1)S(1)}, bf16[3,9,32,128]{3,2,1,0:T(8,128)(2,1)S(1)}, u32[]{:S(2)}, u32[]{:S(2)}) collective-permute-start(bf16[3,9,32,128]{3,2,1,0:T(8,128)(2,1)S(1)} %get-tuple-element.32), channel_id=1, source_target_pairs={{16,0},{24,8},{32,16},{40,24},{48,32},{56,40},{80,64},{88,72},{96,... | collective-permute-start | bytes 663560 | tf_op jit(solution)/shard_map/ppermute | solution.py:315
  126.7 0.0 collective-permute-done.10
  126.7 1.3 collective-permute-start.12
  128.0 0.7 collective-permute-start.11
  128.7 1.1 collective-permute-done.7.from_left
  129.8 2.5 %collective-permute-done.8.from_right = bf16[3,9,32,128]{3,2,1,0:T(8,128)(2,1)S(1)} collective-permute-done((bf16[3,9,32,128]{3,2,1,0:T(8,128)(2,1)S(1)}, bf16[3,9,32,128]{3,2,1,0:T(8,128)(2,1)S(1)}, u32[]{:S(2)}, u32[]{:S(2)}) %collective-permute-start.8) | collective-permute-done | bytes 221216 | tf_op jit(solution)/shard_map/ppermute | solution.py:315
  132.3 1.3 collective-permute-done.12.in_b
  133.6 0.0 collective-permute-done.11.in_a
  133.6 0.0 copy-done.6
  133.6 1.2 gather.1
  134.8 1.9 %collective-permute-start.13 = (bf16[3,4,4,32,128]{4,3,2,1,0:T(8,128)(2,1)S(1)}, bf16[3,4,4,32,128]{4,3,2,1,0:T(8,128)(2,1)S(1)}, u32[]{:S(2)}, u32[]{:S(2)}) collective-permute-start(bf16[3,4,4,32,128]{4,3,2,1,0:T(8,128)(2,1)S(1)} %get-tuple-element.36), channel_id=1, source_target_pairs={{0,8},{8,0},{16,24},{24,16},{32,40},{40,32},{48,56},{56,48},{64,72... | collective-permute-start | bytes 1179656 | tf_op jit(solution)/shard_map/ppermute | solution.py:332
  136.8 1.7 %collective-permute-done.13.got = bf16[3,4,4,32,128]{4,3,2,1,0:T(8,128)(2,1)S(1)} collective-permute-done((bf16[3,4,4,32,128]{4,3,2,1,0:T(8,128)(2,1)S(1)}, bf16[3,4,4,32,128]{4,3,2,1,0:T(8,128)(2,1)S(1)}, u32[]{:S(2)}, u32[]{:S(2)}) %collective-permute-start.13) | collective-permute-done | bytes 393248 | tf_op jit(solution)/shard_map/ppermute | solution.py:332
  138.5 22.5 %all-to-all-done.1.times = bf16[8,48,1024]{2,1,0:T(8,128)(2,1)S(1)} async-done(((bf16[8,48,1024]{2,1,0:T(8,128)(2,1)}), bf16[8,48,1024]{2,1,0:T(8,128)(2,1)S(1)}, u32[]{:S(2)}, u32[]{:S(2)}) %all-to-all-start.1) | async-done | bytes 786464 | tf_op jit(solution)/shard_map/all_to_all | solution.py:335
  161.0 1.7 %final.1 = (bf16[128,1024]{1,0:T(8,128)(2,1)}, bf16[128,1024]{1,0:T(8,128)(2,1)}, bf16[128,1024]{1,0:T(8,128)(2,1)}) custom-call(s32[4]{0:T(128)S(1)} %copy-done.3, bf16[3,4,4,32,128]{4,3,2,1,0:T(8,128)(2,1)S(1)} %get-tuple-element.35.keep, bf16[3,4,4,32,128]{4,3,2,1,0:T(8,128)(2,1)S(1)} %collective-permute-done.13.got, ...), custom_call_target="tpu_custom_call" | custom-call | flops 1048576 | bytes 3145728 | tf_op jit(solution)/shard_map/final/pallas_call | solution.py:381
  (2 shorter events, 0.0 us)
Async XLA Ops:
  0.6 0.7 copy-start
  5.4 4.0 %copy-start.3 = (s32[4]{0:T(128)S(1)}, s32[4]{0:T(128)}, u32[]{:S(2)}) copy-start(s32[4]{0:T(128)} %pad_add_fusion.scal) | copy-start | bytes 52
  5.4 4.0 %collective-permute-start = (bf16[4,4,4,32,128]{4,3,2,1,0:T(8,128)(2,1)}, bf16[4,4,4,32,128]{4,3,2,1,0:T(8,128)(2,1)S(1)}, u32[]{:S(2)}, u32[]{:S(2)}) collective-permute-start(bf16[4,4,4,32,128]{4,3,2,1,0:T(8,128)(2,1)} %get-tuple-element.24), channel_id=1, source_target_pairs={{0,8},{8,0},{16,24},{24,16},{32,40},{40,32},{48,56},{56,48},{64,72... | collective-permute-start | bytes 1572872 | tf_op jit(solution)/shard_map/ppermute | solution.py:332
  9.4 1.0 copy-start.1
  11.1 11.7 %collective-permute-start.3 = (bf16[4,5,32,128]{3,2,1,0:T(8,128)(2,1)S(1)}, bf16[4,5,32,128]{3,2,1,0:T(8,128)(2,1)S(1)}, u32[]{:S(2)}, u32[]{:S(2)}) collective-permute-start(bf16[4,5,32,128]{3,2,1,0:T(8,128)(2,1)S(1)} %get-tuple-element.29), channel_id=1, source_target_pairs={{0,16},{8,24},{48,32},{56,40},{64,80},{72,88},{112,96},{120,104},{... | collective-permute-start | bytes 491528 | tf_op jit(solution)/shard_map/ppermute | solution.py:315
  22.8 27.5 %collective-permute-start.4 = (bf16[4,5,32,128]{3,2,1,0:T(8,128)(2,1)S(1)}, bf16[4,5,32,128]{3,2,1,0:T(8,128)(2,1)}, u32[]{:S(2)}, u32[]{:S(2)}) collective-permute-start(bf16[4,5,32,128]{3,2,1,0:T(8,128)(2,1)S(1)} %broadcast_select_fusion), channel_id=1, source_target_pairs={{0,448},{8,456},{16,464},{24,472},{32,96},{40,104},{48,112},{56,12... | collective-permute-start | bytes 491528 | tf_op jit(solution)/shard_map/ppermute | solution.py:315
  37.5 14.8 %collective-permute-start.1 = (bf16[4,9,32,128]{3,2,1,0:T(8,128)(2,1)S(1)}, bf16[4,9,32,128]{3,2,1,0:T(8,128)(2,1)S(1)}, u32[]{:S(2)}, u32[]{:S(2)}) collective-permute-start(bf16[4,9,32,128]{3,2,1,0:T(8,128)(2,1)S(1)} %get-tuple-element.26), channel_id=1, source_target_pairs={{0,16},{8,24},{16,32},{24,40},{32,48},{40,56},{64,80},{72,88},{80,... | collective-permute-start | bytes 884744 | tf_op jit(solution)/shard_map/ppermute | solution.py:315
  39.4 12.9 %collective-permute-start.2 = (bf16[4,9,32,128]{3,2,1,0:T(8,128)(2,1)S(1)}, bf16[4,9,32,128]{3,2,1,0:T(8,128)(2,1)S(1)}, u32[]{:S(2)}, u32[]{:S(2)}) collective-permute-start(bf16[4,9,32,128]{3,2,1,0:T(8,128)(2,1)S(1)} %get-tuple-element.27), channel_id=1, source_target_pairs={{16,0},{24,8},{32,16},{40,24},{48,32},{56,40},{80,64},{88,72},{96,... | collective-permute-start | bytes 884744 | tf_op jit(solution)/shard_map/ppermute | solution.py:315
  43.3 65.7 %all-to-all-start = ((bf16[8,64,1024]{2,1,0:T(8,128)(2,1)}), bf16[8,64,1024]{2,1,0:T(8,128)(2,1)S(1)}, u32[]{:S(2)}, u32[]{:S(2)}) async-start(bf16[8,64,1024]{2,1,0:T(8,128)(2,1)} %get-tuple-element.38), calls=%async_computation | async-start | bytes 2097152 | tf_op jit(solution)/shard_map/all_to_all | solution.py:335
  50.3 4.5 %collective-permute-start.6 = (bf16[4,5,32,128]{3,2,1,0:T(8,128)(2,1)}, bf16[4,5,32,128]{3,2,1,0:T(8,128)(2,1)S(1)}, u32[]{:S(2)}, u32[]{:S(2)}) collective-permute-start(bf16[4,5,32,128]{3,2,1,0:T(8,128)(2,1)} %collective-permute-done.4), channel_id=1, source_target_pairs={{16,48},{24,56},{32,0},{40,8},{80,112},{88,120},{96,64},{104,72},{... | collective-permute-start | bytes 491528 | tf_op jit(solution)/shard_map/ppermute | solution.py:315
  51.6 3.2 %collective-permute-start.5 = (bf16[4,5,32,128]{3,2,1,0:T(8,128)(2,1)}, bf16[4,5,32,128]{3,2,1,0:T(8,128)(2,1)S(1)}, u32[]{:S(2)}, u32[]{:S(2)}) collective-permute-start(bf16[4,5,32,128]{3,2,1,0:T(8,128)(2,1)} %collective-permute-done.4), channel_id=1, source_target_pairs={{0,48},{8,56},{48,0},{56,8},{64,112},{72,120},{112,64},{120,72},{1... | collective-permute-start | bytes 491528 | tf_op jit(solution)/shard_map/ppermute | solution.py:315
  60.9 0.9 copy-start.5
  61.8 47.2 %copy-start.2 = (f32[64,1024]{1,0:T(8,128)S(1)}, f32[64,1024]{1,0:T(8,128)}, u32[]{:S(2)}) copy-start(f32[64,1024]{1,0:T(8,128)} %table.1) | copy-start | bytes 786436
  61.8 9.8 %collective-permute-start.9 = (bf16[3,5,32,128]{3,2,1,0:T(8,128)(2,1)S(1)}, bf16[3,5,32,128]{3,2,1,0:T(8,128)(2,1)S(1)}, u32[]{:S(2)}, u32[]{:S(2)}) collective-permute-start(bf16[3,5,32,128]{3,2,1,0:T(8,128)(2,1)S(1)} %get-tuple-element.34), channel_id=1, source_target_pairs={{0,16},{8,24},{48,32},{56,40},{64,80},{72,88},{112,96},{120,104},{... | collective-permute-start | bytes 368648 | tf_op jit(solution)/shard_map/ppermute | solution.py:315
  71.6 37.4 %copy-start.4 = (s32[8]{0:T(128)S(1)}, s32[8]{0:T(128)}, u32[]{:S(2)}) copy-start(s32[8]{0:T(128)} %steps.1) | copy-start | bytes 100
  71.6 55.1 %collective-permute-start.10 = (bf16[3,5,32,128]{3,2,1,0:T(8,128)(2,1)S(1)}, bf16[3,5,32,128]{3,2,1,0:T(8,128)(2,1)S(1)}, u32[]{:S(2)}, u32[]{:S(2)}) collective-permute-start(bf16[3,5,32,128]{3,2,1,0:T(8,128)(2,1)S(1)} %broadcast_select_fusion.1), channel_id=1, source_target_pairs={{0,448},{8,456},{16,464},{24,472},{32,96},{40,104},{48,112},{56,12... | collective-permute-start | bytes 368648 | tf_op jit(solution)/shard_map/ppermute | solution.py:315
  114.4 19.2 %copy-start.6 = (bf16[3,4,8,32,128]{4,3,2,1,0:T(8,128)(2,1)S(1)}, bf16[3,4,8,32,128]{4,3,2,1,0:T(8,128)(2,1)}, u32[]{:S(2)}) copy-start(bf16[3,4,8,32,128]{4,3,2,1,0:T(8,128)(2,1)} %copy-done.5) | copy-start | bytes 2359300
  114.4 46.6 %all-to-all-start.1 = ((bf16[8,48,1024]{2,1,0:T(8,128)(2,1)}), bf16[8,48,1024]{2,1,0:T(8,128)(2,1)S(1)}, u32[]{:S(2)}, u32[]{:S(2)}) async-start(bf16[8,48,1024]{2,1,0:T(8,128)(2,1)} %temporal.1), calls=%async_computation.1 | async-start | bytes 1572864 | tf_op jit(solution)/shard_map/all_to_all | solution.py:335
  120.9 9.0 %collective-permute-start.7 = (bf16[3,9,32,128]{3,2,1,0:T(8,128)(2,1)S(1)}, bf16[3,9,32,128]{3,2,1,0:T(8,128)(2,1)S(1)}, u32[]{:S(2)}, u32[]{:S(2)}) collective-permute-start(bf16[3,9,32,128]{3,2,1,0:T(8,128)(2,1)S(1)} %get-tuple-element.31), channel_id=1, source_target_pairs={{0,16},{8,24},{16,32},{24,40},{32,48},{40,56},{64,80},{72,88},{80,... | collective-permute-start | bytes 663560 | tf_op jit(solution)/shard_map/ppermute | solution.py:315
  122.8 9.5 %collective-permute-start.8 = (bf16[3,9,32,128]{3,2,1,0:T(8,128)(2,1)S(1)}, bf16[3,9,32,128]{3,2,1,0:T(8,128)(2,1)S(1)}, u32[]{:S(2)}, u32[]{:S(2)}) collective-permute-start(bf16[3,9,32,128]{3,2,1,0:T(8,128)(2,1)S(1)} %get-tuple-element.32), channel_id=1, source_target_pairs={{16,0},{24,8},{32,16},{40,24},{48,32},{56,40},{80,64},{88,72},{96,... | collective-permute-start | bytes 663560 | tf_op jit(solution)/shard_map/ppermute | solution.py:315
  126.7 6.9 %collective-permute-start.12 = (bf16[3,5,32,128]{3,2,1,0:T(8,128)(2,1)S(1)}, bf16[3,5,32,128]{3,2,1,0:T(8,128)(2,1)S(1)}, u32[]{:S(2)}, u32[]{:S(2)}) collective-permute-start(bf16[3,5,32,128]{3,2,1,0:T(8,128)(2,1)S(1)} %collective-permute-done.10), channel_id=1, source_target_pairs={{16,48},{24,56},{32,0},{40,8},{80,112},{88,120},{96,64},{104,72},{... | collective-permute-start | bytes 368648 | tf_op jit(solution)/shard_map/ppermute | solution.py:315
  128.0 5.6 %collective-permute-start.11 = (bf16[3,5,32,128]{3,2,1,0:T(8,128)(2,1)S(1)}, bf16[3,5,32,128]{3,2,1,0:T(8,128)(2,1)S(1)}, u32[]{:S(2)}, u32[]{:S(2)}) collective-permute-start(bf16[3,5,32,128]{3,2,1,0:T(8,128)(2,1)S(1)} %collective-permute-done.10), channel_id=1, source_target_pairs={{0,48},{8,56},{48,0},{56,8},{64,112},{72,120},{112,64},{120,72},{1... | collective-permute-start | bytes 368648 | tf_op jit(solution)/shard_map/ppermute | solution.py:315
  134.8 3.6 %collective-permute-start.13 = (bf16[3,4,4,32,128]{4,3,2,1,0:T(8,128)(2,1)S(1)}, bf16[3,4,4,32,128]{4,3,2,1,0:T(8,128)(2,1)S(1)}, u32[]{:S(2)}, u32[]{:S(2)}) collective-permute-start(bf16[3,4,4,32,128]{4,3,2,1,0:T(8,128)(2,1)S(1)} %get-tuple-element.36), channel_id=1, source_target_pairs={{0,8},{8,0},{16,24},{24,16},{32,40},{40,32},{48,56},{56,48},{64,72... | collective-permute-start | bytes 1179656 | tf_op jit(solution)/shard_map/ppermute | solution.py:332
where the time goes:
time: 163 us
  waiting for transfers between devices  75.9 us (47%)
  starting transfers between devices  64.2 us (39%)
  Pallas kernels  18.3 us (11%)
  local copies, waits for them, and re-layouts  2.79 us (2%)
    ppermute x12, starting transfers between devices, send(): return lax.ppermute(x, 'lon', moves(by))  48.7 us
    all_to_all x2, waiting for transfers between devices, over_frames(): return lax.all_to_all(x, 'tm', split_axis=0, concat_axis=0, tiled=True)  44.2 us
    ppermute x12, waiting for transfers between devices, send(): return lax.ppermute(x, 'lon', moves(by))  27.9 us
    all_to_all x2, starting transfers between devices, over_frames(): return lax.all_to_all(x, 'tm', split_axis=0, concat_axis=0, tiled=True)  11.7 us
    pallas_call x1, Pallas kernels, shards(): call(spatial_body, [(3, PAIRS, 8, 32, LANES)] + sides(3), [SMEM] + [VMEM]...  6.08 us
    pallas_call x1, Pallas kernels, shards(): call(temporal_body, [(8, 48, 1024)], [SMEM, VMEM, VMEM], TEMPORAL_FLOPS,...  5.43 us
    ppermute x2, starting transfers between devices, core_swap(): return lax.ppermute(x, 'lon', [(i, i ^ 1) for i in range(devices)])  3.84 us
    ppermute x2, waiting for transfers between devices, core_swap(): return lax.ppermute(x, 'lon', [(i, i ^ 1) for i in range(devices)])  3.77 us
  transfers between devices with their start and end apart: 16, of which 11 were waited for; matrix products, arithmetic and copies ran while one was open for 0% of the time, Pallas kernels for 8%

commit v1 on v0

--- a/solution.py
+++ b/solution.py
@@ -17,9 +17,10 @@
 VMEM = pl.BlockSpec(memory_space=pltpu.VMEM)
 SMEM = pl.BlockSpec(memory_space=pltpu.SMEM)
 ANY = pl.BlockSpec(memory_space=pl.ANY)
-SPATIAL_FLOPS = 480 << 26
-TEMPORAL_FLOPS = 1 << 20
-GATHER_FLOPS = 84 << 28
+SPATIAL_FLOPS = 200 << 28
+TEMPORAL_FLOPS = 128 << 28
+HALO_FLOPS = 1 << 28
+GATHER_FLOPS = 1 << 20
 BF16 = jnp.bfloat16
 F32 = jnp.float32
 
@@ -30,10 +31,10 @@
     return sum(jnp.where(b < top, one, zero) for top in (2, 4, 5, 7))
 
 
-def call(body, outs, in_specs, flops, nbytes, scratch=(), mib=48):
+def call(body, outs, in_specs, flops, nbytes, scratch=(), mib=24):
     return pl.pallas_call(
         body,
-        out_shape=[jax.ShapeDtypeStruct(s, BF16) for s in outs],
+        out_shape=[s if isinstance(s, jax.ShapeDtypeStruct) else jax.ShapeDtypeStruct(s, BF16) for s in outs],
         in_specs=in_specs,
         out_specs=[VMEM] * len(outs),
         scratch_shapes=list(scratch),
@@ -98,11 +99,13 @@
             put(r, cross_b[r, slot - HALF])
 
 
-def halo_body(scal, own, got, whole, to_left, to_right, cross_a, cross_b):
+def halo_body(scal, steps, own, got, table, whole, to_left, to_right, cross_a, cross_b, gates):
     b = scal[1]
     core = scal[2]
     first, last = row_end(scal)
     n_low = low_pairs(b)
+    for f in range(8):
+        gates[f] = table[pl.ds(steps[f], 1), :]
     for r in range(4):
         for p in range(PAIRS):
             whole[r, p, pl.ds(core * 4, 4)] = own[r, p]
@@ -266,11 +269,9 @@
             move((1 - core) * 4 + i, send)
 
 
-def temporal_body(steps, arrived, table, out, gates):
+def temporal_body(arrived, gates, out):
     frames = 8
     tokens = frames * 16
-    for f in range(frames):
-        gates[f] = table[pl.ds(steps[f], 1), :]
 
     def spot(dim, shape):
         return lax.broadcasted_iota(jnp.int32, shape, dim) & 15
@@ -300,7 +301,7 @@
                         out[:, lo : lo + LANES] = (space + time).astype(BF16).reshape(128, LANES)
 
 
-def exchange(to_left, to_right, cross_a, cross_b):
+def exchange(to_left, to_right, cross_a, cross_b, late=False):
     devices = lax.axis_size("lon")
     chips = devices // 2
 
@@ -315,13 +316,16 @@
         return lax.ppermute(x, "lon", moves(by))
 
     beside = send(cross_b, {3: -1, 0: 1})
+    if late:
+        to_left, to_right, beside = lax.optimization_barrier((to_left, to_right, beside))
     from_left = send(to_right, {0: 1, 1: 1, 2: 1})
     from_right = send(to_left, {1: -1, 2: -1, 3: -1})
-    column = (lax.axis_index("lon") >> 1) & 3
-    outer = jnp.logical_or(column == 0, column == 3)
-    far = send(jnp.where(outer, cross_a, beside), {3: ROW, 2: ROW, 1: -ROW, 0: -ROW})
-    in_a = send(far, {3: -3, 0: 3})
-    in_b = send(far, {2: -2, 1: 2})
+    if late:
+        cross_a, beside, from_left, from_right = lax.optimization_barrier(
+            (cross_a, beside, from_left, from_right)
+        )
+    in_a = send(cross_a, {3: 1, 0: -1})
+    in_b = send(beside, {2: 2, 1: -2})
     return beside, (from_left, from_right, in_a, in_b)
 
 
@@ -344,34 +348,33 @@
 
     def sides(count):
         side = (count, SLOTS, 32, LANES)
-        return [side, side, (count, HALF, 32, LANES), (count, HALF, 32, LANES)]
+        return [side, side, (count, HALF, 32, LANES), (count, SLOTS - HALF, 32, LANES)]
 
     with jax.named_scope("split"):
         stacked, own, other = call(
             split_body, [(8, 64, 1024), half, half], [SMEM] + [ANY] * 4, 1 << 20, 3 << 20,
             [pltpu.VMEM((4, 128, 1024), BF16), pltpu.SemaphoreType.DMA((4,))], 60,
         )(scal, *flat)
+    arrived = over_frames(stacked)
     got = core_swap(other)
     with jax.named_scope("halo"):
-        whole, *out = call(
-            halo_body, [(4, PAIRS, 8, 32, LANES)] + sides(4), [SMEM] + [VMEM] * 2, 1 << 20, 3 << 20
-        )(scal, own, got)
-    beside, arriving = exchange(*out)
-    stacked, _ = lax.optimization_barrier((stacked, beside))
-    arrived = over_frames(stacked)
+        whole, *out, gates = call(
+            halo_body, [(4, PAIRS, 8, 32, LANES)] + sides(4) + [jax.ShapeDtypeStruct((8, 1, 1024), F32)],
+            [SMEM] * 2 + [VMEM] * 3, HALO_FLOPS, 3 << 20,
+        )(scal, noise_steps, own, got, gate_table)
+    beside, arriving = exchange(*out, late=True)
+    arrived, _ = lax.optimization_barrier((arrived, beside))
+    with jax.named_scope("temporal"):
+        (out_time,) = call(
+            temporal_body, [(8, 48, 1024)], [VMEM, VMEM], TEMPORAL_FLOPS, 4 << 20
+        )(arrived, gates)
+    times = over_frames(out_time)
     with jax.named_scope("spatial"):
         local, *back = call(
             spatial_body, [(3, PAIRS, 8, 32, LANES)] + sides(3), [SMEM] + [VMEM] * 5, SPATIAL_FLOPS, 4 << 20,
             [pltpu.VMEM((4, 8, 32, LANES), BF16), pltpu.VMEM((3, 8, 32, LANES), BF16)],
         )(scal, whole, *arriving)
-    beside, returned = exchange(*back)
-    arrived, _ = lax.optimization_barrier((arrived, beside))
-    with jax.named_scope("temporal"):
-        (out_time,) = call(
-            temporal_body, [(8, 48, 1024)], [SMEM, VMEM, VMEM], TEMPORAL_FLOPS, 4 << 20,
-            [pltpu.VMEM((8, 1, 1024), F32)],
-        )(noise_steps, arrived, gate_table)
-    times = over_frames(out_time)
+    _, returned = exchange(*back)
     with jax.named_scope("gather"):
         keep, send = call(
             gather_body, [(3, PAIRS, 4, 32, LANES)] * 2, [SMEM] + [VMEM] * 5, GATHER_FLOPS, 2 << 20

time: 163 us -> 153 us (0.939)
  the two profiles are of different devices: /device:TPU:2 before, /device:TPU:65 now
where the time goes in v1:
time: 153 us; the launch traced here: 152 us
  starting transfers between devices  74.3 us (49%)
  waiting for transfers between devices  57 us (37%)
  Pallas kernels  18.6 us (12%)
    ppermute x10, starting transfers between devices, send(): return lax.ppermute(x, 'lon', moves(by))  40.8 us
    ppermute x10, waiting for transfers between devices, send(): return lax.ppermute(x, 'lon', moves(by))  36.1 us
    all_to_all x2, starting transfers between devices, over_frames(): return lax.all_to_all(x, 'tm', split_axis=0, concat_axis=0, tiled=True)  27.8 us
    all_to_all x2, waiting for transfers between devices, over_frames(): return lax.all_to_all(x, 'tm', split_axis=0, concat_axis=0, tiled=True)  18 us
    pallas_call x1, Pallas kernels, shards(): call(spatial_body, [(3, PAIRS, 8, 32, LANES)] + sides(3), [SMEM] + [VMEM]...  6.39 us
    ppermute x2, starting transfers between devices, core_swap(): return lax.ppermute(x, 'lon', [(i, i ^ 1) for i in range(devices)])  5.73 us
    pallas_call x1, Pallas kernels, shards(): call(temporal_body, [(8, 48, 1024)], [VMEM, VMEM], TEMPORAL_FLOPS, 4 << 20)  4.88 us
    pallas_call x1, Pallas kernels, shards(): call(split_body, [(8, 64, 1024), half, half], [SMEM] + [ANY] * 4, 1 << 20...  3.27 us
  transfers between devices with their start and end apart: 14, of which 7 were waited for; matrix products, arithmetic and copies ran while one was open for 0% of the time, Pallas kernels for 9%

profile of v1, /device:TPU:65, one launch (start us, length us, event | category | flops | bytes accessed | tf_op | source)
XLA Modules:
  0.0 152.3 jit_solution(10156190214699270700)
XLA Ops:
  0.6 0.0 copy-start
  0.7 0.7 copy-done
  1.3 0.2 dynamic-slice_reduce_fusion
  1.5 0.6 pad_add_fusion.scal
  2.1 3.3 %split.1 = (bf16[8,64,1024]{2,1,0:T(8,128)(2,1)}, bf16[4,4,4,32,128]{4,3,2,1,0:T(8,128)(2,1)}, bf16[4,4,4,32,128]{4,3,2,1,0:T(8,128)(2,1)}) custom-call(s32[4]{0:T(128)} %pad_add_fusion.scal, bf16[128,1024]{1,0:T(8,128)(2,1)} %bitcast.9, bf16[128,1024]{1,0:T(8,128)(2,1)} %bitcast.10, bf16[128,1024]{1,0:T(8,128)(2,1)} %bitcast.11, bf16[128,1024]{1,0:T(8,128)(2,1)} %bitcast.12), custom_call_target="tpu_custom_call" | custom-call | flops 1048576 | bytes 3145728 | tf_op jit(solution)/shard_map/split/pallas_call | solution.py:354
  5.4 0.0 copy-start.5
  5.4 0.0 copy-start.1
  5.4 0.0 copy-start.2
  5.4 11.8 %all-to-all-start = ((bf16[8,64,1024]{2,1,0:T(8,128)(2,1)}), bf16[8,64,1024]{2,1,0:T(8,128)(2,1)S(1)}, u32[]{:S(2)}, u32[]{:S(2)}) async-start(bf16[8,64,1024]{2,1,0:T(8,128)(2,1)} %get-tuple-element.51), calls=%async_computation | async-start | bytes 2097152 | tf_op jit(solution)/shard_map/all_to_all | solution.py:339
  17.2 0.0 copy-done.5
  17.2 0.0 copy-start.3
  17.2 0.0 copy-start.4
  17.2 3.3 %collective-permute-start = (bf16[4,4,4,32,128]{4,3,2,1,0:T(8,128)(2,1)S(1)}, bf16[4,4,4,32,128]{4,3,2,1,0:T(8,128)(2,1)S(1)}, u32[]{:S(2)}, u32[]{:S(2)}) collective-permute-start(bf16[4,4,4,32,128]{4,3,2,1,0:T(8,128)(2,1)S(1)} %copy-done.5), channel_id=1, source_target_pairs={{0,8},{8,0},{16,24},{24,16},{32,40},{40,32},{48,56},{56,48},{64,72... | collective-permute-start | bytes 1572872 | tf_op jit(solution)/shard_map/ppermute | solution.py:336
  20.5 1.5 collective-permute-done.got
  22.0 0.0 copy-done.1
  22.0 0.0 copy-done.2
  22.0 0.0 copy-done.3
  22.0 0.0 copy-done.4
  22.0 1.0 halo.1
  23.0 3.1 %collective-permute-start.1 = (bf16[4,4,32,128]{3,2,1,0:T(8,128)(2,1)S(1)}, bf16[4,4,32,128]{3,2,1,0:T(8,128)(2,1)S(1)}, u32[]{:S(2)}, u32[]{:S(2)}) collective-permute-start(bf16[4,4,32,128]{3,2,1,0:T(8,128)(2,1)S(1)} %get-tuple-element.36), channel_id=1, source_target_pairs={{0,16},{8,24},{48,32},{56,40},{64,80},{72,88},{112,96},{120,104},{... | collective-permute-start | bytes 393224 | tf_op jit(solution)/shard_map/ppermute | solution.py:316
  26.1 2.5 %collective-permute-done.1 = bf16[4,4,32,128]{3,2,1,0:T(8,128)(2,1)S(1)} collective-permute-done((bf16[4,4,32,128]{3,2,1,0:T(8,128)(2,1)S(1)}, bf16[4,4,32,128]{3,2,1,0:T(8,128)(2,1)S(1)}, u32[]{:S(2)}, u32[]{:S(2)}) %collective-permute-start.1) | collective-permute-done | bytes 131104 | tf_op jit(solution)/shard_map/ppermute | solution.py:316
  28.5 4.1 %collective-permute-start.2 = (bf16[4,9,32,128]{3,2,1,0:T(8,128)(2,1)S(1)}, bf16[4,9,32,128]{3,2,1,0:T(8,128)(2,1)S(1)}, u32[]{:S(2)}, u32[]{:S(2)}) collective-permute-start(bf16[4,9,32,128]{3,2,1,0:T(8,128)(2,1)S(1)} %get-tuple-element.38), channel_id=1, source_target_pairs={{0,16},{8,24},{16,32},{24,40},{32,48},{40,56},{64,80},{72,88},{80,... | collective-permute-start | bytes 884744 | tf_op jit(solution)/shard_map/ppermute | solution.py:316
  32.7 1.3 collective-permute-start.3
  34.0 3.7 %collective-permute-done.2.from_left = bf16[4,9,32,128]{3,2,1,0:T(8,128)(2,1)S(1)} collective-permute-done((bf16[4,9,32,128]{3,2,1,0:T(8,128)(2,1)S(1)}, bf16[4,9,32,128]{3,2,1,0:T(8,128)(2,1)S(1)}, u32[]{:S(2)}, u32[]{:S(2)}) %collective-permute-start.2) | collective-permute-done | bytes 294944 | tf_op jit(solution)/shard_map/ppermute | solution.py:316
  37.7 3.8 %collective-permute-done.3.from_right = bf16[4,9,32,128]{3,2,1,0:T(8,128)(2,1)S(1)} collective-permute-done((bf16[4,9,32,128]{3,2,1,0:T(8,128)(2,1)S(1)}, bf16[4,9,32,128]{3,2,1,0:T(8,128)(2,1)S(1)}, u32[]{:S(2)}, u32[]{:S(2)}) %collective-permute-start.3) | collective-permute-done | bytes 294944 | tf_op jit(solution)/shard_map/ppermute | solution.py:316
  41.6 1.3 collective-permute-start.5
  42.9 10.0 %collective-permute-start.4 = (bf16[4,5,32,128]{3,2,1,0:T(8,128)(2,1)S(1)}, bf16[4,5,32,128]{3,2,1,0:T(8,128)(2,1)S(1)}, u32[]{:S(2)}, u32[]{:S(2)}) collective-permute-start(bf16[4,5,32,128]{3,2,1,0:T(8,128)(2,1)S(1)} %get-tuple-element.42), channel_id=1, source_target_pairs={{0,496},{8,504},{48,64},{56,72},{64,48},{72,56},{112,128},{120,136... | collective-permute-start | bytes 491528 | tf_op jit(solution)/shard_map/ppermute | solution.py:316
  52.9 18.0 %all-to-all-done.arrived = bf16[8,64,1024]{2,1,0:T(8,128)(2,1)S(1)} async-done(((bf16[8,64,1024]{2,1,0:T(8,128)(2,1)}), bf16[8,64,1024]{2,1,0:T(8,128)(2,1)S(1)}, u32[]{:S(2)}, u32[]{:S(2)}) %all-to-all-start) | async-done | bytes 1048608 | tf_op jit(solution)/shard_map/all_to_all | solution.py:339
  70.9 4.9 %temporal.1 = bf16[8,48,1024]{2,1,0:T(8,128)(2,1)} custom-call(bf16[8,64,1024]{2,1,0:T(8,128)(2,1)S(1)} %all-to-all-done.arrived, f32[8,1,1024]{2,1,0:T(1,128)S(1)} %get-tuple-element.53.gates), custom_call_target="tpu_custom_call" | custom-call | flops 34359738368 | bytes 4194304 | tf_op jit(solution)/shard_map/temporal/pallas_call | solution.py:368
  75.8 16.0 %all-to-all-start.1 = ((bf16[8,48,1024]{2,1,0:T(8,128)(2,1)}), bf16[8,48,1024]{2,1,0:T(8,128)(2,1)S(1)}, u32[]{:S(2)}, u32[]{:S(2)}) async-start(bf16[8,48,1024]{2,1,0:T(8,128)(2,1)} %temporal.1), calls=%async_computation.1 | async-start | bytes 1572864 | tf_op jit(solution)/shard_map/all_to_all | solution.py:339
  91.8 0.0 collective-permute-done.5.in_b
  91.8 0.0 collective-permute-done.4.in_a
  91.8 6.4 %spatial.1 = (bf16[3,4,8,32,128]{4,3,2,1,0:T(8,128)(2,1)S(1)}, bf16[3,9,32,128]{3,2,1,0:T(8,128)(2,1)S(1)}, bf16[3,9,32,128]{3,2,1,0:T(8,128)(2,1)S(1)}, bf16[3,...) custom-call(s32[4]{0:T(128)S(1)} %copy-done.3, bf16[4,4,8,32,128]{4,3,2,1,0:T(8,128)(2,1)S(1)} %get-tuple-element.32.whole, ...), custom_call_target="tpu_custom_call" | custom-call | flops 53687091200 | bytes 4194304 | tf_op jit(solution)/shard_map/spatial/pallas_call | solution.py:373
  98.2 1.3 collective-permute-start.6
  99.5 1.3 collective-permute-start.7
  100.8 4.0 %collective-permute-start.9 = (bf16[3,4,32,128]{3,2,1,0:T(8,128)(2,1)S(1)}, bf16[3,4,32,128]{3,2,1,0:T(8,128)(2,1)S(1)}, u32[]{:S(2)}, u32[]{:S(2)}) collective-permute-start(bf16[3,4,32,128]{3,2,1,0:T(8,128)(2,1)S(1)} %get-tuple-element.48), channel_id=1, source_target_pairs={{0,16},{8,24},{48,32},{56,40},{64,80},{72,88},{112,96},{120,104},{... | collective-permute-start | bytes 294920 | tf_op jit(solution)/shard_map/ppermute | solution.py:316
  104.8 13.2 %collective-permute-start.8 = (bf16[3,5,32,128]{3,2,1,0:T(8,128)(2,1)S(1)}, bf16[3,5,32,128]{3,2,1,0:T(8,128)(2,1)S(1)}, u32[]{:S(2)}, u32[]{:S(2)}) collective-permute-start(bf16[3,5,32,128]{3,2,1,0:T(8,128)(2,1)S(1)} %get-tuple-element.47), channel_id=1, source_target_pairs={{0,496},{8,504},{48,64},{56,72},{64,48},{72,56},{112,128},{120,136... | collective-permute-start | bytes 368648 | tf_op jit(solution)/shard_map/ppermute | solution.py:316
  118.0 0.0 collective-permute-done.9
  118.0 1.3 collective-permute-start.10
  119.3 26.1 %collective-permute-done.8.in_a = bf16[3,5,32,128]{3,2,1,0:T(8,128)(2,1)S(1)} collective-permute-done((bf16[3,5,32,128]{3,2,1,0:T(8,128)(2,1)S(1)}, bf16[3,5,32,128]{3,2,1,0:T(8,128)(2,1)S(1)}, u32[]{:S(2)}, u32[]{:S(2)}) %collective-permute-start.8) | collective-permute-done | bytes 122912 | tf_op jit(solution)/shard_map/ppermute | solution.py:316
  145.4 0.0 collective-permute-done.10.in_b
  145.4 0.0 collective-permute-done.6.from_left
  145.4 0.0 collective-permute-done.7.from_right
  145.4 1.4 gather.1
  146.8 2.5 %collective-permute-start.11 = (bf16[3,4,4,32,128]{4,3,2,1,0:T(8,128)(2,1)S(1)}, bf16[3,4,4,32,128]{4,3,2,1,0:T(8,128)(2,1)S(1)}, u32[]{:S(2)}, u32[]{:S(2)}) collective-permute-start(bf16[3,4,4,32,128]{4,3,2,1,0:T(8,128)(2,1)S(1)} %get-tuple-element.50), channel_id=1, source_target_pairs={{0,8},{8,0},{16,24},{24,16},{32,40},{40,32},{48,56},{56,48},{64,72... | collective-permute-start | bytes 1179656 | tf_op jit(solution)/shard_map/ppermute | solution.py:336
  149.3 1.3 collective-permute-done.11.got
  150.6 0.0 all-to-all-done.1.times
  150.6 1.7 %final.1 = (bf16[128,1024]{1,0:T(8,128)(2,1)}, bf16[128,1024]{1,0:T(8,128)(2,1)}, bf16[128,1024]{1,0:T(8,128)(2,1)}) custom-call(s32[4]{0:T(128)S(1)} %copy-done.3, bf16[3,4,4,32,128]{4,3,2,1,0:T(8,128)(2,1)S(1)} %get-tuple-element.49.keep, bf16[3,4,4,32,128]{4,3,2,1,0:T(8,128)(2,1)S(1)} %collective-permute-done.11.got, ...), custom_call_target="tpu_custom_call" | custom-call | flops 1048576 | bytes 3145728 | tf_op jit(solution)/shard_map/final/pallas_call | solution.py:384
Async XLA Ops:
  0.6 0.7 copy-start
  5.4 11.8 %copy-start.5 = (bf16[4,4,4,32,128]{4,3,2,1,0:T(8,128)(2,1)S(1)}, bf16[4,4,4,32,128]{4,3,2,1,0:T(8,128)(2,1)}, u32[]{:S(2)}) copy-start(bf16[4,4,4,32,128]{4,3,2,1,0:T(8,128)(2,1)} %get-tuple-element.31) | copy-start | bytes 1572868
  5.4 16.6 %copy-start.1 = (bf16[4,4,4,32,128]{4,3,2,1,0:T(8,128)(2,1)S(1)}, bf16[4,4,4,32,128]{4,3,2,1,0:T(8,128)(2,1)}, u32[]{:S(2)}) copy-start(bf16[4,4,4,32,128]{4,3,2,1,0:T(8,128)(2,1)} %get-tuple-element.30.own) | copy-start | bytes 1572868
  5.4 16.6 %copy-start.2 = (f32[64,1024]{1,0:T(8,128)S(1)}, f32[64,1024]{1,0:T(8,128)}, u32[]{:S(2)}) copy-start(f32[64,1024]{1,0:T(8,128)} %table.1) | copy-start | bytes 786436
  5.4 65.5 %all-to-all-start = ((bf16[8,64,1024]{2,1,0:T(8,128)(2,1)}), bf16[8,64,1024]{2,1,0:T(8,128)(2,1)S(1)}, u32[]{:S(2)}, u32[]{:S(2)}) async-start(bf16[8,64,1024]{2,1,0:T(8,128)(2,1)} %get-tuple-element.51), calls=%async_computation | async-start | bytes 2097152 | tf_op jit(solution)/shard_map/all_to_all | solution.py:339
  17.2 4.8 %copy-start.3 = (s32[4]{0:T(128)S(1)}, s32[4]{0:T(128)}, u32[]{:S(2)}) copy-start(s32[4]{0:T(128)} %pad_add_fusion.scal) | copy-start | bytes 52
  17.2 4.8 %copy-start.4 = (s32[8]{0:T(128)S(1)}, s32[8]{0:T(128)}, u32[]{:S(2)}) copy-start(s32[8]{0:T(128)} %steps.1) | copy-start | bytes 100
  17.2 4.8 %collective-permute-start = (bf16[4,4,4,32,128]{4,3,2,1,0:T(8,128)(2,1)S(1)}, bf16[4,4,4,32,128]{4,3,2,1,0:T(8,128)(2,1)S(1)}, u32[]{:S(2)}, u32[]{:S(2)}) collective-permute-start(bf16[4,4,4,32,128]{4,3,2,1,0:T(8,128)(2,1)S(1)} %copy-done.5), channel_id=1, source_target_pairs={{0,8},{8,0},{16,24},{24,16},{32,40},{40,32},{48,56},{56,48},{64,72... | collective-permute-start | bytes 1572872 | tf_op jit(solution)/shard_map/ppermute | solution.py:336
  23.0 5.6 %collective-permute-start.1 = (bf16[4,4,32,128]{3,2,1,0:T(8,128)(2,1)S(1)}, bf16[4,4,32,128]{3,2,1,0:T(8,128)(2,1)S(1)}, u32[]{:S(2)}, u32[]{:S(2)}) collective-permute-start(bf16[4,4,32,128]{3,2,1,0:T(8,128)(2,1)S(1)} %get-tuple-element.36), channel_id=1, source_target_pairs={{0,16},{8,24},{48,32},{56,40},{64,80},{72,88},{112,96},{120,104},{... | collective-permute-start | bytes 393224 | tf_op jit(solution)/shard_map/ppermute | solution.py:316
  28.5 9.2 %collective-permute-start.2 = (bf16[4,9,32,128]{3,2,1,0:T(8,128)(2,1)S(1)}, bf16[4,9,32,128]{3,2,1,0:T(8,128)(2,1)S(1)}, u32[]{:S(2)}, u32[]{:S(2)}) collective-permute-start(bf16[4,9,32,128]{3,2,1,0:T(8,128)(2,1)S(1)} %get-tuple-element.38), channel_id=1, source_target_pairs={{0,16},{8,24},{16,32},{24,40},{32,48},{40,56},{64,80},{72,88},{80,... | collective-permute-start | bytes 884744 | tf_op jit(solution)/shard_map/ppermute | solution.py:316
  32.7 8.9 %collective-permute-start.3 = (bf16[4,9,32,128]{3,2,1,0:T(8,128)(2,1)S(1)}, bf16[4,9,32,128]{3,2,1,0:T(8,128)(2,1)S(1)}, u32[]{:S(2)}, u32[]{:S(2)}) collective-permute-start(bf16[4,9,32,128]{3,2,1,0:T(8,128)(2,1)S(1)} %get-tuple-element.39), channel_id=1, source_target_pairs={{16,0},{24,8},{32,16},{40,24},{48,32},{56,40},{80,64},{88,72},{96,... | collective-permute-start | bytes 884744 | tf_op jit(solution)/shard_map/ppermute | solution.py:316
  41.6 50.2 %collective-permute-start.5 = (bf16[4,4,32,128]{3,2,1,0:T(8,128)(2,1)S(1)}, bf16[4,4,32,128]{3,2,1,0:T(8,128)(2,1)S(1)}, u32[]{:S(2)}, u32[]{:S(2)}) collective-permute-start(bf16[4,4,32,128]{3,2,1,0:T(8,128)(2,1)S(1)} %collective-permute-done.1), channel_id=1, source_target_pairs={{16,496},{24,504},{32,64},{40,72},{80,48},{88,56},{96,128},{104,13... | collective-permute-start | bytes 393224 | tf_op jit(solution)/shard_map/ppermute | solution.py:316
  42.9 49.0 %collective-permute-start.4 = (bf16[4,5,32,128]{3,2,1,0:T(8,128)(2,1)S(1)}, bf16[4,5,32,128]{3,2,1,0:T(8,128)(2,1)S(1)}, u32[]{:S(2)}, u32[]{:S(2)}) collective-permute-start(bf16[4,5,32,128]{3,2,1,0:T(8,128)(2,1)S(1)} %get-tuple-element.42), channel_id=1, source_target_pairs={{0,496},{8,504},{48,64},{56,72},{64,48},{72,56},{112,128},{120,136... | collective-permute-start | bytes 491528 | tf_op jit(solution)/shard_map/ppermute | solution.py:316
  75.8 74.8 %all-to-all-start.1 = ((bf16[8,48,1024]{2,1,0:T(8,128)(2,1)}), bf16[8,48,1024]{2,1,0:T(8,128)(2,1)S(1)}, u32[]{:S(2)}, u32[]{:S(2)}) async-start(bf16[8,48,1024]{2,1,0:T(8,128)(2,1)} %temporal.1), calls=%async_computation.1 | async-start | bytes 1572864 | tf_op jit(solution)/shard_map/all_to_all | solution.py:339
  98.2 47.2 %collective-permute-start.6 = (bf16[3,9,32,128]{3,2,1,0:T(8,128)(2,1)S(1)}, bf16[3,9,32,128]{3,2,1,0:T(8,128)(2,1)S(1)}, u32[]{:S(2)}, u32[]{:S(2)}) collective-permute-start(bf16[3,9,32,128]{3,2,1,0:T(8,128)(2,1)S(1)} %get-tuple-element.45), channel_id=1, source_target_pairs={{0,16},{8,24},{16,32},{24,40},{32,48},{40,56},{64,80},{72,88},{80,... | collective-permute-start | bytes 663560 | tf_op jit(solution)/shard_map/ppermute | solution.py:316
  99.5 45.8 %collective-permute-start.7 = (bf16[3,9,32,128]{3,2,1,0:T(8,128)(2,1)S(1)}, bf16[3,9,32,128]{3,2,1,0:T(8,128)(2,1)S(1)}, u32[]{:S(2)}, u32[]{:S(2)}) collective-permute-start(bf16[3,9,32,128]{3,2,1,0:T(8,128)(2,1)S(1)} %get-tuple-element.46), channel_id=1, source_target_pairs={{16,0},{24,8},{32,16},{40,24},{48,32},{56,40},{80,64},{88,72},{96,... | collective-permute-start | bytes 663560 | tf_op jit(solution)/shard_map/ppermute | solution.py:316
  100.8 17.2 %collective-permute-start.9 = (bf16[3,4,32,128]{3,2,1,0:T(8,128)(2,1)S(1)}, bf16[3,4,32,128]{3,2,1,0:T(8,128)(2,1)S(1)}, u32[]{:S(2)}, u32[]{:S(2)}) collective-permute-start(bf16[3,4,32,128]{3,2,1,0:T(8,128)(2,1)S(1)} %get-tuple-element.48), channel_id=1, source_target_pairs={{0,16},{8,24},{48,32},{56,40},{64,80},{72,88},{112,96},{120,104},{... | collective-permute-start | bytes 294920 | tf_op jit(solution)/shard_map/ppermute | solution.py:316
  104.8 40.5 %collective-permute-start.8 = (bf16[3,5,32,128]{3,2,1,0:T(8,128)(2,1)S(1)}, bf16[3,5,32,128]{3,2,1,0:T(8,128)(2,1)S(1)}, u32[]{:S(2)}, u32[]{:S(2)}) collective-permute-start(bf16[3,5,32,128]{3,2,1,0:T(8,128)(2,1)S(1)} %get-tuple-element.47), channel_id=1, source_target_pairs={{0,496},{8,504},{48,64},{56,72},{64,48},{72,56},{112,128},{120,136... | collective-permute-start | bytes 368648 | tf_op jit(solution)/shard_map/ppermute | solution.py:316
  118.0 27.4 %collective-permute-start.10 = (bf16[3,4,32,128]{3,2,1,0:T(8,128)(2,1)S(1)}, bf16[3,4,32,128]{3,2,1,0:T(8,128)(2,1)S(1)}, u32[]{:S(2)}, u32[]{:S(2)}) collective-permute-start(bf16[3,4,32,128]{3,2,1,0:T(8,128)(2,1)S(1)} %collective-permute-done.9), channel_id=1, source_target_pairs={{16,496},{24,504},{32,64},{40,72},{80,48},{88,56},{96,128},{104,13... | collective-permute-start | bytes 294920 | tf_op jit(solution)/shard_map/ppermute | solution.py:316
  146.8 3.8 %collective-permute-start.11 = (bf16[3,4,4,32,128]{4,3,2,1,0:T(8,128)(2,1)S(1)}, bf16[3,4,4,32,128]{4,3,2,1,0:T(8,128)(2,1)S(1)}, u32[]{:S(2)}, u32[]{:S(2)}) collective-permute-start(bf16[3,4,4,32,128]{4,3,2,1,0:T(8,128)(2,1)S(1)} %get-tuple-element.50), channel_id=1, source_target_pairs={{0,8},{8,0},{16,24},{24,16},{32,40},{40,32},{48,56},{56,48},{64,72... | collective-permute-start | bytes 1179656 | tf_op jit(solution)/shard_map/ppermute | solution.py:336

commit v2 on v1

--- a/solution.py
+++ b/solution.py
@@ -20,6 +20,7 @@
 SPATIAL_FLOPS = 200 << 28
 TEMPORAL_FLOPS = 128 << 28
 HALO_FLOPS = 1 << 28
+SIDES_FLOPS = 1 << 20
 GATHER_FLOPS = 1 << 20
 BF16 = jnp.bfloat16
 F32 = jnp.float32
@@ -43,15 +44,23 @@
     )
 
 
-def split_body(scal, q, k, v, g, stacked, own, other, held, sems):
-    core = scal[2]
-    copies = [pltpu.make_async_copy(ref, held.at[r], sems.at[r]) for r, ref in enumerate((q, k, v, g))]
-    for copy in copies:
-        copy.start()
-    for r, copy in enumerate(copies):
-        copy.wait()
-        for i in range(8):
-            stacked[i, 16 * r : 16 * r + 16, :] = held[r, 16 * i : 16 * i + 16, :]
+def split_body(q, k, v, g, stacked, own, other, sems):
+    core = lax.axis_index("lon") & 1
+    copies = [
+        [
+            pltpu.make_async_copy(
+                ref.at[pl.ds(16 * i, 16)], stacked.at[i, pl.ds(16 * r, 16)], sems.at[r, i]
+            )
+            for i in range(8)
+        ]
+        for r, ref in enumerate((q, k, v, g))
+    ]
+    for row in copies:
+        for copy in row:
+            copy.start()
+    for r, row in enumerate(copies):
+        for copy in row:
+            copy.wait()
         for half in range(2):
 
             @pl.when(core == half)
@@ -59,18 +68,16 @@
                 for p in range(PAIRS):
                     lo = half * PAIRS * LANES + p * LANES
                     hi = (1 - half) * PAIRS * LANES + p * LANES
-                    own[r, p] = held[r, :, lo : lo + LANES].reshape(4, 32, LANES)
-                    other[r, p] = held[r, :, hi : hi + LANES].reshape(4, 32, LANES)
+                    rows = slice(16 * r, 16 * r + 16)
+                    own[r, p] = stacked[:, rows, lo : lo + LANES].reshape(4, 32, LANES)
+                    other[r, p] = stacked[:, rows, hi : hi + LANES].reshape(4, 32, LANES)
 
 
 def row_end(scal):
     return scal[3] == 0, scal[3] == 3
 
 
-def store_block(slot, count, block, side, cross_a, cross_b, crosses):
-    for r in range(count):
-        side[r, slot] = block(r)
-
+def store_cross(slot, count, block, cross_a, cross_b, crosses):
     @pl.when(jnp.logical_and(crosses, slot < HALF))
     def _():
         for r in range(count):
@@ -115,8 +122,9 @@
         @pl.when(p < n_low)
         def _(p=p):
             def put(col, carry):
-                block = lambda r: whole[r, p, col]
-                store_block(p * b + col, 4, block, to_left, cross_a, cross_b, first)
+                for r in range(4):
+                    to_left[r, p * b + col] = whole[r, p, col]
+                store_cross(p * b + col, 4, lambda r: whole[r, p, col], cross_a, cross_b, first)
                 return carry
 
             lax.fori_loop(0, b, put, 0)
@@ -124,9 +132,10 @@
         @pl.when(p >= n_low)
         def _(p=p):
             def put(col, carry):
-                block = lambda r: whole[r, p, col]
                 slot = (p - n_low) * (8 - b) + col - b
-                store_block(slot, 4, block, to_right, cross_a, cross_b, last)
+                for r in range(4):
+                    to_right[r, slot] = whole[r, p, col]
+                store_cross(slot, 4, lambda r: whole[r, p, col], cross_a, cross_b, last)
                 return carry
 
             lax.fori_loop(b, 8, put, 0)
@@ -142,25 +151,22 @@
     g2 = jnp.concatenate([g * first, g * second], axis=0)
     over_last = (((1,), (1,)), ((), ()))
     over_first = (((0,), (0,)), ((), ()))
-    s = lax.dot_general(q2, k, over_last, preferred_element_type=F32)
-    dp = lax.dot_general(g2, v, over_last, preferred_element_type=F32)
+    s = lax.dot_general(k, q2, over_last, preferred_element_type=F32)
+    dp = lax.dot_general(v, g2, over_last, preferred_element_type=F32)
     s = jnp.where(mask, s, NEG)
-    e = jnp.exp(s - jnp.max(s, axis=1, keepdims=True))
-    p = e * (1.0 / jnp.sum(e, axis=1, keepdims=True))
-    delta = jnp.sum(p * dp, axis=1, keepdims=True)
+    e = jnp.exp(s - jnp.max(s, axis=0, keepdims=True))
+    p = e * (1.0 / jnp.sum(e, axis=0, keepdims=True))
+    delta = jnp.sum(p * dp, axis=0, keepdims=True)
     ds = (p * (dp - delta)).astype(BF16)
     p = p.astype(BF16)
-    dv = lax.dot_general(p, g2, over_first, preferred_element_type=F32)
-    dk = lax.dot_general(ds, q2, over_first, preferred_element_type=F32)
-    dq = jnp.dot(ds[:tokens], k * first, preferred_element_type=F32)
-    dq = dq + jnp.dot(ds[tokens:], k * second, preferred_element_type=F32)
+    dv = jnp.dot(p, g2, preferred_element_type=F32)
+    dk = jnp.dot(ds, q2, preferred_element_type=F32)
+    dq = lax.dot_general(ds[:, :tokens], k * first, over_first, preferred_element_type=F32)
+    dq = dq + lax.dot_general(ds[:, tokens:], k * second, over_first, preferred_element_type=F32)
     return (dq * SCALE, dk, dv)
 
 
-def spatial_body(
-    scal, whole, from_left, from_right, in_a, in_b,
-    local, back_left, back_right, out_a, out_b, strip, grads,
-):
+def spatial_body(scal, whole, from_left, from_right, in_a, in_b, strips, out_a, out_b, strip):
     a = scal[0]
     b = scal[1]
     first, last = row_end(scal)
@@ -171,67 +177,87 @@
         row = lax.broadcasted_iota(jnp.int32, shape, dim) & 31
         return (row + WIN - a) >> 3
 
-    mask = block_of(0, (2 * tokens, tokens)) == block_of(1, (2 * tokens, tokens))
-
-    def per_pair(p, carry):
+    mask = block_of(0, (tokens, 2 * tokens)) == block_of(1, (tokens, 2 * tokens))
+
+    for p in range(PAIRS):
         low = p < n_low
 
-        def place(col):
-            here = jnp.logical_xor(low, col < b)
-            there = jnp.logical_not(here)
-            on_right = jnp.logical_and(there, low)
-            on_left = jnp.logical_and(there, jnp.logical_not(low))
-            return here, on_left, on_right, p * b + col, (p - n_low) * (8 - b) + col - b
-
-        def fetch(col, inner):
-            here, on_left, on_right, slot_right, slot_left = place(col)
-
-            def put(r, block):
-                strip[r, col] = block
-
-            @pl.when(here)
-            def _():
+        def slot_of(col, p=p):
+            return p * b + col, (p - n_low) * (8 - b) + col - b
+
+        @pl.when(low)
+        def _(p=p):
+            def here(col, carry):
                 for r in range(4):
-                    strip[r, col] = whole[r, p, col]
-
-            @pl.when(on_right)
-            def _():
-                load_block(slot_right, 4, put, from_right, in_a, in_b, last)
-
-            @pl.when(on_left)
-            def _():
-                load_block(slot_left, 4, put, from_left, in_a, in_b, first)
-
-            return inner
-
-        lax.fori_loop(0, 8, fetch, 0)
-        q, k, v, g = (strip[r].reshape(tokens, LANES) for r in range(4))
+                    strip[p, r, col] = whole[r, p, col]
+                return carry
+
+            def there(col, carry):
+                def put(r, block):
+                    strip[p, r, col] = block
+
+                load_block(slot_of(col)[0], 4, put, from_right, in_a, in_b, last)
+                return carry
+
+            lax.fori_loop(b, 8, here, 0)
+            lax.fori_loop(0, b, there, 0)
+
+        @pl.when(jnp.logical_not(low))
+        def _(p=p):
+            def here(col, carry):
+                for r in range(4):
+                    strip[p, r, col] = whole[r, p, col]
+                return carry
+
+            def there(col, carry):
+                def put(r, block):
+                    strip[p, r, col] = block
+
+                load_block(slot_of(col)[1], 4, put, from_left, in_a, in_b, first)
+                return carry
+
+            lax.fori_loop(0, b, here, 0)
+            lax.fori_loop(b, 8, there, 0)
+
+    for p in range(PAIRS):
+        q, k, v, g = (strip[p, r].reshape(tokens, LANES) for r in range(4))
         for r, grad in enumerate(attend(q, k, v, g, mask)):
-            grads[r] = grad.astype(BF16).reshape(8, 32, LANES)
-
-        def store(col, inner):
-            here, on_left, on_right, slot_right, slot_left = place(col)
-            block = lambda r: grads[r, col]
-
-            @pl.when(here)
-            def _():
+            strips[r, p] = grad.astype(BF16).reshape(8, 32, LANES)
+
+    for p in range(PAIRS):
+        low = p < n_low
+
+        def out(col, carry, p=p, low=low):
+            block = lambda r: strips[r, p, col]
+            slot = jnp.where(low, p * b + col, (p - n_low) * (8 - b) + col - b)
+            store_cross(slot, 3, block, out_a, out_b, jnp.where(low, scal[3], 3 - scal[3]) == 3)
+            return carry
+
+        lax.fori_loop(jnp.where(low, 0, b), jnp.where(low, b, 8), out, 0)
+
+
+def sides_body(scal, strips, back_left, back_right):
+    b = scal[1]
+    n_low = low_pairs(b)
+    for p in range(PAIRS):
+
+        @pl.when(p < n_low)
+        def _(p=p):
+            def put(col, carry):
                 for r in range(3):
-                    local[r, p, col] = grads[r, col]
-
-            @pl.when(on_right)
-            def _():
-                store_block(slot_right, 3, block, back_right, out_a, out_b, last)
-
-            @pl.when(on_left)
-            def _():
-                store_block(slot_left, 3, block, back_left, out_a, out_b, first)
-
-            return inner
-
-        lax.fori_loop(0, 8, store, 0)
-        return carry
-
-    lax.fori_loop(0, PAIRS, per_pair, 0)
+                    back_right[r, p * b + col] = strips[r, p, col]
+                return carry
+
+            lax.fori_loop(0, b, put, 0)
+
+        @pl.when(p >= n_low)
+        def _(p=p):
+            def put(col, carry):
+                for r in range(3):
+                    back_left[r, (p - n_low) * (8 - b) + col - b] = strips[r, p, col]
+                return carry
+
+            lax.fori_loop(b, 8, put, 0)
 
 
 def gather_body(scal, local, from_left, from_right, in_a, in_b, keep, send):
@@ -276,7 +302,7 @@
     def spot(dim, shape):
         return lax.broadcasted_iota(jnp.int32, shape, dim) & 15
 
-    mask = spot(0, (2 * tokens, tokens)) == spot(1, (2 * tokens, tokens))
+    mask = spot(0, (tokens, 2 * tokens)) == spot(1, (tokens, 2 * tokens))
     for p in range(8):
         lanes = slice(p * LANES, (p + 1) * LANES)
         q, k, v, g = (arrived[:, 16 * r : 16 * r + 16, lanes] for r in range(4))
@@ -301,32 +327,25 @@
                         out[:, lo : lo + LANES] = (space + time).astype(BF16).reshape(128, LANES)
 
 
-def exchange(to_left, to_right, cross_a, cross_b, late=False):
+def send(x, by):
     devices = lax.axis_size("lon")
     chips = devices // 2
-
-    def moves(by):
-        return [
-            (i, ((i // 2 + by[i // 2 % ROW]) % chips) * 2 + i % 2)
-            for i in range(devices)
-            if i // 2 % ROW in by
-        ]
-
-    def send(x, by):
-        return lax.ppermute(x, "lon", moves(by))
-
-    beside = send(cross_b, {3: -1, 0: 1})
-    if late:
-        to_left, to_right, beside = lax.optimization_barrier((to_left, to_right, beside))
-    from_left = send(to_right, {0: 1, 1: 1, 2: 1})
-    from_right = send(to_left, {1: -1, 2: -1, 3: -1})
-    if late:
-        cross_a, beside, from_left, from_right = lax.optimization_barrier(
-            (cross_a, beside, from_left, from_right)
-        )
-    in_a = send(cross_a, {3: 1, 0: -1})
-    in_b = send(beside, {2: 2, 1: -2})
-    return beside, (from_left, from_right, in_a, in_b)
+    moves = [
+        (i, ((i // 2 + by[i // 2 % ROW]) % chips) * 2 + i % 2) for i in range(devices) if i // 2 % ROW in by
+    ]
+    return lax.ppermute(x, "lon", moves)
+
+
+def scatter_row(cross_b):
+    return send(cross_b, {3: -1, 0: 1})
+
+
+def cross_rows(cross_a, beside):
+    return send(cross_a, {3: 1, 0: -1}), send(beside, {2: 2, 1: -2})
+
+
+def in_row(to_left, to_right):
+    return send(to_right, {0: 1, 1: 1, 2: 1}), send(to_left, {1: -1, 2: -1, 3: -1})
 
 
 def shards(queries, token_keys, values, grad_out, window_shifts, noise_steps, gate_table):
@@ -352,9 +371,9 @@
 
     with jax.named_scope("split"):
         stacked, own, other = call(
-            split_body, [(8, 64, 1024), half, half], [SMEM] + [ANY] * 4, 1 << 20, 3 << 20,
-            [pltpu.VMEM((4, 128, 1024), BF16), pltpu.SemaphoreType.DMA((4,))], 60,
-        )(scal, *flat)
+            split_body, [(8, 64, 1024), half, half], [ANY] * 4, 1 << 20, 3 << 20,
+            [pltpu.SemaphoreType.DMA((4, 8))], 60,
+        )(*flat)
     arrived = over_frames(stacked)
     got = core_swap(other)
     with jax.named_scope("halo"):
@@ -362,7 +381,12 @@
             halo_body, [(4, PAIRS, 8, 32, LANES)] + sides(4) + [jax.ShapeDtypeStruct((8, 1, 1024), F32)],
             [SMEM] * 2 + [VMEM] * 3, HALO_FLOPS, 3 << 20,
         )(scal, noise_steps, own, got, gate_table)
-    beside, arriving = exchange(*out, late=True)
+    to_left, to_right, cross_a, cross_b = out
+    beside = scatter_row(cross_b)
+    to_left, to_right, beside = lax.optimization_barrier((to_left, to_right, beside))
+    from_left, from_right = in_row(to_left, to_right)
+    cross_a, beside, from_left, from_right = lax.optimization_barrier((cross_a, beside, from_left, from_right))
+    in_a, in_b = cross_rows(cross_a, beside)
     arrived, _ = lax.optimization_barrier((arrived, beside))
     with jax.named_scope("temporal"):
         (out_time,) = call(
@@ -370,15 +394,20 @@
         )(arrived, gates)
     times = over_frames(out_time)
     with jax.named_scope("spatial"):
-        local, *back = call(
-            spatial_body, [(3, PAIRS, 8, 32, LANES)] + sides(3), [SMEM] + [VMEM] * 5, SPATIAL_FLOPS, 4 << 20,
-            [pltpu.VMEM((4, 8, 32, LANES), BF16), pltpu.VMEM((3, 8, 32, LANES), BF16)],
-        )(scal, whole, *arriving)
-    _, returned = exchange(*back)
+        strips, out_a, out_b = call(
+            spatial_body, [(3, PAIRS, 8, 32, LANES)] + sides(3)[2:], [SMEM] + [VMEM] * 5, SPATIAL_FLOPS, 4 << 20,
+            [pltpu.VMEM((PAIRS, 4, 8, 32, LANES), BF16)],
+        )(scal, whole, from_left, from_right, in_a, in_b)
+    beside = scatter_row(out_b)
+    out_a, beside = lax.optimization_barrier((out_a, beside))
+    in_a, in_b = cross_rows(out_a, beside)
+    with jax.named_scope("sides"):
+        back_left, back_right = call(sides_body, sides(3)[:2], [SMEM, VMEM], SIDES_FLOPS, 1 << 20)(scal, strips)
+    from_left, from_right = in_row(back_left, back_right)
     with jax.named_scope("gather"):
         keep, send = call(
             gather_body, [(3, PAIRS, 4, 32, LANES)] * 2, [SMEM] + [VMEM] * 5, GATHER_FLOPS, 2 << 20
-        )(scal, local, *returned)
+        )(scal, strips, from_left, from_right, in_a, in_b)
     got_back = core_swap(send)
     with jax.named_scope("final"):
         outs = call(final_body, [(128, 1024)] * 3, [SMEM] + [VMEM] * 3, 1 << 20, 3 << 20)(

time: 153 us -> 149 us (0.974)
  Pallas kernels: 18.6 us -> 15 us
  waiting for transfers between devices: 57 us -> 58.9 us
    ppermute x10, waiting for transfers between devices: 36.1 us -> 38.7 us  [send(): return lax.ppermute(x, 'lon', moves)]
    pallas_call x2 -> x3, Pallas kernels: 9.67 us -> 7.16 us  [the longest x1 3.68 us: shards(): call(spatial_body, [(3, PAIRS, 8, 32, LANES)] + sides(3)[2:], [SMEM] + [V...]
    pallas_call x1, Pallas kernels: 4.88 us -> 3.28 us  [shards(): call(temporal_body, [(8, 48, 1024)], [VMEM, VMEM], TEMPORAL_FLOPS, 4 << 20)]
  transfers between devices with their start and end apart: 14 -> 14, of which waited for: 7 -> 8; matrix products, arithmetic and copies ran while one was open for 0% -> 0% of each run, Pallas kernels for 9% -> 7%
where the time goes in v2:
time: 149 us
  starting transfers between devices  73.6 us (49%)
  waiting for transfers between devices  58.9 us (40%)
  Pallas kernels  15 us (10%)
    ppermute x10, starting transfers between devices, send(): return lax.ppermute(x, 'lon', moves)  40.3 us
    ppermute x10, waiting for transfers between devices, send(): return lax.ppermute(x, 'lon', moves)  38.7 us
    all_to_all x2, starting transfers between devices, over_frames(): return lax.all_to_all(x, 'tm', split_axis=0, concat_axis=0, tiled=True)  27.8 us
    all_to_all x2, waiting for transfers between devices, over_frames(): return lax.all_to_all(x, 'tm', split_axis=0, concat_axis=0, tiled=True)  17.6 us
    ppermute x2, starting transfers between devices, core_swap(): return lax.ppermute(x, 'lon', [(i, i ^ 1) for i in range(devices)])  5.59 us
    pallas_call x1, Pallas kernels, shards(): call(spatial_body, [(3, PAIRS, 8, 32, LANES)] + sides(3)[2:], [SMEM] + [V...  3.68 us
    pallas_call x1, Pallas kernels, shards(): call(temporal_body, [(8, 48, 1024)], [VMEM, VMEM], TEMPORAL_FLOPS, 4 << 20)  3.28 us
  transfers between devices with their start and end apart: 14, of which 8 were waited for; matrix products, arithmetic and copies ran while one was open for 0% of the time, Pallas kernels for 7%

profile of v2, /device:TPU:65, one launch (start us, length us, event | category | flops | bytes accessed | tf_op | source)
XLA Modules:
  0.0 148.7 jit_solution(17404667819500212905)
XLA Ops:
  0.6 0.0 copy-start
  0.6 2.8 %split.1 = (bf16[8,64,1024]{2,1,0:T(8,128)(2,1)}, bf16[4,4,4,32,128]{4,3,2,1,0:T(8,128)(2,1)}, bf16[4,4,4,32,128]{4,3,2,1,0:T(8,128)(2,1)}) custom-call(bf16[128,1024]{1,0:T(8,128)(2,1)} %bitcast.9, bf16[128,1024]{1,0:T(8,128)(2,1)} %bitcast.10, bf16[128,1024]{1,0:T(8,128)(2,1)} %bitcast.11, bf16[128,1024]{1,0:T(8,128)(2,1)} %bitcast.12), custom_call_target="tpu_custom_call" | custom-call | flops 1048576 | bytes 3145728 | tf_op jit(solution)/shard_map/split/pallas_call | solution.py:373
  3.5 0.0 copy-start.4
  3.5 0.0 copy-start.1
  3.5 0.0 copy-start.2
  3.5 11.8 %all-to-all-start = ((bf16[8,64,1024]{2,1,0:T(8,128)(2,1)}), bf16[8,64,1024]{2,1,0:T(8,128)(2,1)S(1)}, u32[]{:S(2)}, u32[]{:S(2)}) async-start(bf16[8,64,1024]{2,1,0:T(8,128)(2,1)} %get-tuple-element.55), calls=%async_computation | async-start | bytes 2097152 | tf_op jit(solution)/shard_map/all_to_all | solution.py:358
  15.3 0.0 copy-done.4
  15.3 3.1 %collective-permute-start = (bf16[4,4,4,32,128]{4,3,2,1,0:T(8,128)(2,1)S(1)}, bf16[4,4,4,32,128]{4,3,2,1,0:T(8,128)(2,1)S(1)}, u32[]{:S(2)}, u32[]{:S(2)}) collective-permute-start(bf16[4,4,4,32,128]{4,3,2,1,0:T(8,128)(2,1)S(1)} %copy-done.4), channel_id=1, source_target_pairs={{0,8},{8,0},{16,24},{24,16},{32,40},{40,32},{48,56},{56,48},{64,72... | collective-permute-start | bytes 1572872 | tf_op jit(solution)/shard_map/ppermute | solution.py:355
  18.4 0.0 copy-done
  18.4 0.2 dynamic-slice_reduce_fusion
  18.6 0.1 pad_add_fusion.scal
  18.7 0.0 copy-start.3
  18.7 1.2 collective-permute-done.got
  19.9 0.0 copy-done.1
  19.9 0.0 copy-done.2
  19.9 0.0 copy-done.3
  19.9 1.5 %halo.1 = (bf16[4,4,8,32,128]{4,3,2,1,0:T(8,128)(2,1)S(1)}, bf16[4,9,32,128]{3,2,1,0:T(8,128)(2,1)S(1)}, bf16[4,9,32,128]{3,2,1,0:T(8,128)(2,1)S(1)}, bf16[4,5,3...) custom-call(s32[4]{0:T(128)S(1)} %pad_add_fusion.scal, s32[8]{0:T(128)S(1)} %copy-done.3, ...), custom_call_target="tpu_custom_call" | custom-call | flops 268435456 | bytes 3145728 | tf_op jit(solution)/shard_map/halo/pallas_call | solution.py:380
  21.5 3.1 %collective-permute-start.1 = (bf16[4,4,32,128]{3,2,1,0:T(8,128)(2,1)S(1)}, bf16[4,4,32,128]{3,2,1,0:T(8,128)(2,1)S(1)}, u32[]{:S(2)}, u32[]{:S(2)}) collective-permute-start(bf16[4,4,32,128]{3,2,1,0:T(8,128)(2,1)S(1)} %get-tuple-element.38), channel_id=1, source_target_pairs={{0,16},{8,24},{48,32},{56,40},{64,80},{72,88},{112,96},{120,104},{... | collective-permute-start | bytes 393224 | tf_op jit(solution)/shard_map/ppermute | solution.py:336
  24.6 2.5 %collective-permute-done.1 = bf16[4,4,32,128]{3,2,1,0:T(8,128)(2,1)S(1)} collective-permute-done((bf16[4,4,32,128]{3,2,1,0:T(8,128)(2,1)S(1)}, bf16[4,4,32,128]{3,2,1,0:T(8,128)(2,1)S(1)}, u32[]{:S(2)}, u32[]{:S(2)}) %collective-permute-start.1) | collective-permute-done | bytes 131104 | tf_op jit(solution)/shard_map/ppermute | solution.py:336
  27.1 4.1 %collective-permute-start.2 = (bf16[4,9,32,128]{3,2,1,0:T(8,128)(2,1)S(1)}, bf16[4,9,32,128]{3,2,1,0:T(8,128)(2,1)S(1)}, u32[]{:S(2)}, u32[]{:S(2)}) collective-permute-start(bf16[4,9,32,128]{3,2,1,0:T(8,128)(2,1)S(1)} %get-tuple-element.40), channel_id=1, source_target_pairs={{0,16},{8,24},{16,32},{24,40},{32,48},{40,56},{64,80},{72,88},{80,... | collective-permute-start | bytes 884744 | tf_op jit(solution)/shard_map/ppermute | solution.py:336
  31.2 1.3 collective-permute-start.3
  32.5 3.7 %collective-permute-done.2.from_left = bf16[4,9,32,128]{3,2,1,0:T(8,128)(2,1)S(1)} collective-permute-done((bf16[4,9,32,128]{3,2,1,0:T(8,128)(2,1)S(1)}, bf16[4,9,32,128]{3,2,1,0:T(8,128)(2,1)S(1)}, u32[]{:S(2)}, u32[]{:S(2)}) %collective-permute-start.2) | collective-permute-done | bytes 294944 | tf_op jit(solution)/shard_map/ppermute | solution.py:336
  36.2 3.8 %collective-permute-done.3.from_right = bf16[4,9,32,128]{3,2,1,0:T(8,128)(2,1)S(1)} collective-permute-done((bf16[4,9,32,128]{3,2,1,0:T(8,128)(2,1)S(1)}, bf16[4,9,32,128]{3,2,1,0:T(8,128)(2,1)S(1)}, u32[]{:S(2)}, u32[]{:S(2)}) %collective-permute-start.3) | collective-permute-done | bytes 294944 | tf_op jit(solution)/shard_map/ppermute | solution.py:336
  40.1 1.3 collective-permute-start.5
  41.4 10.0 %collective-permute-start.4 = (bf16[4,5,32,128]{3,2,1,0:T(8,128)(2,1)}, bf16[4,5,32,128]{3,2,1,0:T(8,128)(2,1)S(1)}, u32[]{:S(2)}, u32[]{:S(2)}) collective-permute-start(bf16[4,5,32,128]{3,2,1,0:T(8,128)(2,1)} %get-tuple-element.44), channel_id=1, source_target_pairs={{0,496},{8,504},{48,64},{56,72},{64,48},{72,56},{112,128},{120,136... | collective-permute-start | bytes 491528 | tf_op jit(solution)/shard_map/ppermute | solution.py:336
  51.4 17.6 %all-to-all-done.arrived = bf16[8,64,1024]{2,1,0:T(8,128)(2,1)S(1)} async-done(((bf16[8,64,1024]{2,1,0:T(8,128)(2,1)}), bf16[8,64,1024]{2,1,0:T(8,128)(2,1)S(1)}, u32[]{:S(2)}, u32[]{:S(2)}) %all-to-all-start) | async-done | bytes 1048608 | tf_op jit(solution)/shard_map/all_to_all | solution.py:358
  69.0 3.3 %temporal.1 = bf16[8,48,1024]{2,1,0:T(8,128)(2,1)} custom-call(bf16[8,64,1024]{2,1,0:T(8,128)(2,1)S(1)} %all-to-all-done.arrived, f32[8,1,1024]{2,1,0:T(1,128)S(1)} %get-tuple-element.57.gates), custom_call_target="tpu_custom_call" | custom-call | flops 34359738368 | bytes 4194304 | tf_op jit(solution)/shard_map/temporal/pallas_call | solution.py:392
  72.3 16.0 %all-to-all-start.1 = ((bf16[8,48,1024]{2,1,0:T(8,128)(2,1)}), bf16[8,48,1024]{2,1,0:T(8,128)(2,1)S(1)}, u32[]{:S(2)}, u32[]{:S(2)}) async-start(bf16[8,48,1024]{2,1,0:T(8,128)(2,1)} %temporal.1), calls=%async_computation.1 | async-start | bytes 1572864 | tf_op jit(solution)/shard_map/all_to_all | solution.py:358
  88.3 0.0 collective-permute-done.5.in_b
  88.3 0.0 collective-permute-done.4.in_a
  88.3 3.7 %spatial.1 = (bf16[3,4,8,32,128]{4,3,2,1,0:T(8,128)(2,1)S(1)}, bf16[3,5,32,128]{3,2,1,0:T(8,128)(2,1)S(1)}, bf16[3,4,32,128]{3,2,1,0:T(8,128)(2,1)S(1)}) custom-call(s32[4]{0:T(128)S(1)} %pad_add_fusion.scal, bf16[4,4,8,32,128]{4,3,2,1,0:T(8,128)(2,1)S(1)} %get-tuple-element.34.whole, bf16[4,9,32,128]{3,2,1,0:T(8,128)(2,1)S(1)} %collective-permute-done.2.from_left, ...), custom_call_target="tpu_custom_call" | custom-call | flops 53687091200 | bytes 4194304 | tf_op jit(solution)/shard_map/spatial/pallas_call | solution.py:397
  92.0 1.3 collective-permute-start.8
  93.3 0.7 sides.1
  93.9 1.3 collective-permute-start.6
  95.3 1.3 collective-permute-start.7
  96.6 0.0 collective-permute-done.8
  96.6 15.3 %collective-permute-start.9 = (bf16[3,5,32,128]{3,2,1,0:T(8,128)(2,1)S(1)}, bf16[3,5,32,128]{3,2,1,0:T(8,128)(2,1)S(1)}, u32[]{:S(2)}, u32[]{:S(2)}) collective-permute-start(bf16[3,5,32,128]{3,2,1,0:T(8,128)(2,1)S(1)} %get-tuple-element.51), channel_id=1, source_target_pairs={{0,496},{8,504},{48,64},{56,72},{64,48},{72,56},{112,128},{120,136... | collective-permute-start | bytes 368648 | tf_op jit(solution)/shard_map/ppermute | solution.py:336
  111.9 1.3 collective-permute-start.10
  113.2 20.5 %collective-permute-done.10.in_b = bf16[3,4,32,128]{3,2,1,0:T(8,128)(2,1)S(1)} collective-permute-done((bf16[3,4,32,128]{3,2,1,0:T(8,128)(2,1)S(1)}, bf16[3,4,32,128]{3,2,1,0:T(8,128)(2,1)S(1)}, u32[]{:S(2)}, u32[]{:S(2)}) %collective-permute-start.10) | collective-permute-done | bytes 98336 | tf_op jit(solution)/shard_map/ppermute | solution.py:336
  133.7 0.0 collective-permute-done.6.from_left
  133.7 0.0 collective-permute-done.7.from_right
  133.7 8.1 %collective-permute-done.9.in_a = bf16[3,5,32,128]{3,2,1,0:T(8,128)(2,1)S(1)} collective-permute-done((bf16[3,5,32,128]{3,2,1,0:T(8,128)(2,1)S(1)}, bf16[3,5,32,128]{3,2,1,0:T(8,128)(2,1)S(1)}, u32[]{:S(2)}, u32[]{:S(2)}) %collective-permute-start.9) | collective-permute-done | bytes 122912 | tf_op jit(solution)/shard_map/ppermute | solution.py:336
  141.9 1.4 gather.1
  143.2 2.5 %collective-permute-start.11 = (bf16[3,4,4,32,128]{4,3,2,1,0:T(8,128)(2,1)S(1)}, bf16[3,4,4,32,128]{4,3,2,1,0:T(8,128)(2,1)S(1)}, u32[]{:S(2)}, u32[]{:S(2)}) collective-permute-start(bf16[3,4,4,32,128]{4,3,2,1,0:T(8,128)(2,1)S(1)} %get-tuple-element.54), channel_id=1, source_target_pairs={{0,8},{8,0},{16,24},{24,16},{32,40},{40,32},{48,56},{56,48},{64,72... | collective-permute-start | bytes 1179656 | tf_op jit(solution)/shard_map/ppermute | solution.py:355
  145.7 1.3 collective-permute-done.11.got
  147.0 0.0 all-to-all-done.1.times
  147.0 1.7 %final.1 = (bf16[128,1024]{1,0:T(8,128)(2,1)}, bf16[128,1024]{1,0:T(8,128)(2,1)}, bf16[128,1024]{1,0:T(8,128)(2,1)}) custom-call(s32[4]{0:T(128)S(1)} %pad_add_fusion.scal, bf16[3,4,4,32,128]{4,3,2,1,0:T(8,128)(2,1)S(1)} %get-tuple-element.53.keep, bf16[3,4,4,32,128]{4,3,2,1,0:T(8,128)(2,1)S(1)} %collective-permute-done.11.got, ...), custom_call_target="tpu_custom_call" | custom-call | flops 1048576 | bytes 3145728 | tf_op jit(solution)/shard_map/final/pallas_call | solution.py:413
Async XLA Ops:
  0.6 17.8 %copy-start = (s32[8,2]{0,1:T(2,128)S(1)}, s32[8,2]{0,1:T(2,128)}, u32[]{:S(2)}) copy-start(s32[8,2]{0,1:T(2,128)} %param.11) | copy-start | bytes 196
  3.5 11.8 %copy-start.4 = (bf16[4,4,4,32,128]{4,3,2,1,0:T(8,128)(2,1)S(1)}, bf16[4,4,4,32,128]{4,3,2,1,0:T(8,128)(2,1)}, u32[]{:S(2)}) copy-start(bf16[4,4,4,32,128]{4,3,2,1,0:T(8,128)(2,1)} %get-tuple-element.33) | copy-start | bytes 1572868
  3.5 16.4 %copy-start.1 = (bf16[4,4,4,32,128]{4,3,2,1,0:T(8,128)(2,1)S(1)}, bf16[4,4,4,32,128]{4,3,2,1,0:T(8,128)(2,1)}, u32[]{:S(2)}) copy-start(bf16[4,4,4,32,128]{4,3,2,1,0:T(8,128)(2,1)} %get-tuple-element.32.own) | copy-start | bytes 1572868
  3.5 16.4 %copy-start.2 = (f32[64,1024]{1,0:T(8,128)S(1)}, f32[64,1024]{1,0:T(8,128)}, u32[]{:S(2)}) copy-start(f32[64,1024]{1,0:T(8,128)} %table.1) | copy-start | bytes 786436
  3.5 65.5 %all-to-all-start = ((bf16[8,64,1024]{2,1,0:T(8,128)(2,1)}), bf16[8,64,1024]{2,1,0:T(8,128)(2,1)S(1)}, u32[]{:S(2)}, u32[]{:S(2)}) async-start(bf16[8,64,1024]{2,1,0:T(8,128)(2,1)} %get-tuple-element.55), calls=%async_computation | async-start | bytes 2097152 | tf_op jit(solution)/shard_map/all_to_all | solution.py:358
  15.3 4.7 %collective-permute-start = (bf16[4,4,4,32,128]{4,3,2,1,0:T(8,128)(2,1)S(1)}, bf16[4,4,4,32,128]{4,3,2,1,0:T(8,128)(2,1)S(1)}, u32[]{:S(2)}, u32[]{:S(2)}) collective-permute-start(bf16[4,4,4,32,128]{4,3,2,1,0:T(8,128)(2,1)S(1)} %copy-done.4), channel_id=1, source_target_pairs={{0,8},{8,0},{16,24},{24,16},{32,40},{40,32},{48,56},{56,48},{64,72... | collective-permute-start | bytes 1572872 | tf_op jit(solution)/shard_map/ppermute | solution.py:355
  18.7 1.2 copy-start.3
  21.5 5.6 %collective-permute-start.1 = (bf16[4,4,32,128]{3,2,1,0:T(8,128)(2,1)S(1)}, bf16[4,4,32,128]{3,2,1,0:T(8,128)(2,1)S(1)}, u32[]{:S(2)}, u32[]{:S(2)}) collective-permute-start(bf16[4,4,32,128]{3,2,1,0:T(8,128)(2,1)S(1)} %get-tuple-element.38), channel_id=1, source_target_pairs={{0,16},{8,24},{48,32},{56,40},{64,80},{72,88},{112,96},{120,104},{... | collective-permute-start | bytes 393224 | tf_op jit(solution)/shard_map/ppermute | solution.py:336
  27.1 9.2 %collective-permute-start.2 = (bf16[4,9,32,128]{3,2,1,0:T(8,128)(2,1)S(1)}, bf16[4,9,32,128]{3,2,1,0:T(8,128)(2,1)S(1)}, u32[]{:S(2)}, u32[]{:S(2)}) collective-permute-start(bf16[4,9,32,128]{3,2,1,0:T(8,128)(2,1)S(1)} %get-tuple-element.40), channel_id=1, source_target_pairs={{0,16},{8,24},{16,32},{24,40},{32,48},{40,56},{64,80},{72,88},{80,... | collective-permute-start | bytes 884744 | tf_op jit(solution)/shard_map/ppermute | solution.py:336
  31.2 8.9 %collective-permute-start.3 = (bf16[4,9,32,128]{3,2,1,0:T(8,128)(2,1)S(1)}, bf16[4,9,32,128]{3,2,1,0:T(8,128)(2,1)S(1)}, u32[]{:S(2)}, u32[]{:S(2)}) collective-permute-start(bf16[4,9,32,128]{3,2,1,0:T(8,128)(2,1)S(1)} %get-tuple-element.41), channel_id=1, source_target_pairs={{16,0},{24,8},{32,16},{40,24},{48,32},{56,40},{80,64},{88,72},{96,... | collective-permute-start | bytes 884744 | tf_op jit(solution)/shard_map/ppermute | solution.py:336
  40.1 48.2 %collective-permute-start.5 = (bf16[4,4,32,128]{3,2,1,0:T(8,128)(2,1)S(1)}, bf16[4,4,32,128]{3,2,1,0:T(8,128)(2,1)S(1)}, u32[]{:S(2)}, u32[]{:S(2)}) collective-permute-start(bf16[4,4,32,128]{3,2,1,0:T(8,128)(2,1)S(1)} %collective-permute-done.1), channel_id=1, source_target_pairs={{16,496},{24,504},{32,64},{40,72},{80,48},{88,56},{96,128},{104,13... | collective-permute-start | bytes 393224 | tf_op jit(solution)/shard_map/ppermute | solution.py:336
  41.4 46.9 %collective-permute-start.4 = (bf16[4,5,32,128]{3,2,1,0:T(8,128)(2,1)}, bf16[4,5,32,128]{3,2,1,0:T(8,128)(2,1)S(1)}, u32[]{:S(2)}, u32[]{:S(2)}) collective-permute-start(bf16[4,5,32,128]{3,2,1,0:T(8,128)(2,1)} %get-tuple-element.44), channel_id=1, source_target_pairs={{0,496},{8,504},{48,64},{56,72},{64,48},{72,56},{112,128},{120,136... | collective-permute-start | bytes 491528 | tf_op jit(solution)/shard_map/ppermute | solution.py:336
  72.3 74.7 %all-to-all-start.1 = ((bf16[8,48,1024]{2,1,0:T(8,128)(2,1)}), bf16[8,48,1024]{2,1,0:T(8,128)(2,1)S(1)}, u32[]{:S(2)}, u32[]{:S(2)}) async-start(bf16[8,48,1024]{2,1,0:T(8,128)(2,1)} %temporal.1), calls=%async_computation.1 | async-start | bytes 1572864 | tf_op jit(solution)/shard_map/all_to_all | solution.py:358
  92.0 4.6 %collective-permute-start.8 = (bf16[3,4,32,128]{3,2,1,0:T(8,128)(2,1)S(1)}, bf16[3,4,32,128]{3,2,1,0:T(8,128)(2,1)S(1)}, u32[]{:S(2)}, u32[]{:S(2)}) collective-permute-start(bf16[3,4,32,128]{3,2,1,0:T(8,128)(2,1)S(1)} %get-tuple-element.50), channel_id=1, source_target_pairs={{0,16},{8,24},{48,32},{56,40},{64,80},{72,88},{112,96},{120,104},{... | collective-permute-start | bytes 294920 | tf_op jit(solution)/shard_map/ppermute | solution.py:336
  93.9 39.8 %collective-permute-start.6 = (bf16[3,9,32,128]{3,2,1,0:T(8,128)(2,1)S(1)}, bf16[3,9,32,128]{3,2,1,0:T(8,128)(2,1)S(1)}, u32[]{:S(2)}, u32[]{:S(2)}) collective-permute-start(bf16[3,9,32,128]{3,2,1,0:T(8,128)(2,1)S(1)} %get-tuple-element.47), channel_id=1, source_target_pairs={{0,16},{8,24},{16,32},{24,40},{32,48},{40,56},{64,80},{72,88},{80,... | collective-permute-start | bytes 663560 | tf_op jit(solution)/shard_map/ppermute | solution.py:336
  95.3 38.5 %collective-permute-start.7 = (bf16[3,9,32,128]{3,2,1,0:T(8,128)(2,1)S(1)}, bf16[3,9,32,128]{3,2,1,0:T(8,128)(2,1)S(1)}, u32[]{:S(2)}, u32[]{:S(2)}) collective-permute-start(bf16[3,9,32,128]{3,2,1,0:T(8,128)(2,1)S(1)} %get-tuple-element.48), channel_id=1, source_target_pairs={{16,0},{24,8},{32,16},{40,24},{48,32},{56,40},{80,64},{88,72},{96,... | collective-permute-start | bytes 663560 | tf_op jit(solution)/shard_map/ppermute | solution.py:336
  96.6 45.3 %collective-permute-start.9 = (bf16[3,5,32,128]{3,2,1,0:T(8,128)(2,1)S(1)}, bf16[3,5,32,128]{3,2,1,0:T(8,128)(2,1)S(1)}, u32[]{:S(2)}, u32[]{:S(2)}) collective-permute-start(bf16[3,5,32,128]{3,2,1,0:T(8,128)(2,1)S(1)} %get-tuple-element.51), channel_id=1, source_target_pairs={{0,496},{8,504},{48,64},{56,72},{64,48},{72,56},{112,128},{120,136... | collective-permute-start | bytes 368648 | tf_op jit(solution)/shard_map/ppermute | solution.py:336
  111.9 21.8 %collective-permute-start.10 = (bf16[3,4,32,128]{3,2,1,0:T(8,128)(2,1)S(1)}, bf16[3,4,32,128]{3,2,1,0:T(8,128)(2,1)S(1)}, u32[]{:S(2)}, u32[]{:S(2)}) collective-permute-start(bf16[3,4,32,128]{3,2,1,0:T(8,128)(2,1)S(1)} %collective-permute-done.8), channel_id=1, source_target_pairs={{16,496},{24,504},{32,64},{40,72},{80,48},{88,56},{96,128},{104,13... | collective-permute-start | bytes 294920 | tf_op jit(solution)/shard_map/ppermute | solution.py:336
  143.2 3.8 %collective-permute-start.11 = (bf16[3,4,4,32,128]{4,3,2,1,0:T(8,128)(2,1)S(1)}, bf16[3,4,4,32,128]{4,3,2,1,0:T(8,128)(2,1)S(1)}, u32[]{:S(2)}, u32[]{:S(2)}) collective-permute-start(bf16[3,4,4,32,128]{4,3,2,1,0:T(8,128)(2,1)S(1)} %get-tuple-element.54), channel_id=1, source_target_pairs={{0,8},{8,0},{16,24},{24,16},{32,40},{40,32},{48,56},{56,48},{64,72... | collective-permute-start | bytes 1179656 | tf_op jit(solution)/shard_map/ppermute | solution.py:355

commit v3 on v2

--- a/solution.py
+++ b/solution.py
@@ -385,7 +385,6 @@
     beside = scatter_row(cross_b)
     to_left, to_right, beside = lax.optimization_barrier((to_left, to_right, beside))
     from_left, from_right = in_row(to_left, to_right)
-    cross_a, beside, from_left, from_right = lax.optimization_barrier((cross_a, beside, from_left, from_right))
     in_a, in_b = cross_rows(cross_a, beside)
     arrived, _ = lax.optimization_barrier((arrived, beside))
     with jax.named_scope("temporal"):

time: 149 us -> 149 us (level)
  waiting for transfers between devices: 58.9 us -> 53.4 us
  starting transfers between devices: 73.6 us -> 78.9 us
    ppermute x10, waiting for transfers between devices: 38.7 us -> 28.7 us  [send(): return lax.ppermute(x, 'lon', moves)]
    ppermute x10, starting transfers between devices: 40.3 us -> 45.6 us  [send(): return lax.ppermute(x, 'lon', moves)]
    all_to_all x2, waiting for transfers between devices: 17.6 us -> 22.2 us  [over_frames(): return lax.all_to_all(x, 'tm', split_axis=0, concat_axis=0, tiled=True)]
  transfers between devices with their start and end apart: 14 -> 14, of which waited for: 8 -> 5; matrix products, arithmetic and copies ran while one was open for 0% -> 0% of each run, Pallas kernels for 7% -> 7%
where the time goes in v3:
time: 149 us
  starting transfers between devices  78.9 us (53%)
  waiting for transfers between devices  53.4 us (36%)
  Pallas kernels  15.2 us (10%)
    ppermute x10, starting transfers between devices, send(): return lax.ppermute(x, 'lon', moves)  45.6 us
    ppermute x10, waiting for transfers between devices, send(): return lax.ppermute(x, 'lon', moves)  28.7 us
    all_to_all x2, starting transfers between devices, over_frames(): return lax.all_to_all(x, 'tm', split_axis=0, concat_axis=0, tiled=True)  27.8 us
    all_to_all x2, waiting for transfers between devices, over_frames(): return lax.all_to_all(x, 'tm', split_axis=0, concat_axis=0, tiled=True)  22.2 us
    ppermute x2, starting transfers between devices, core_swap(): return lax.ppermute(x, 'lon', [(i, i ^ 1) for i in range(devices)])  5.59 us
    pallas_call x1, Pallas kernels, shards(): call(spatial_body, [(3, PAIRS, 8, 32, LANES)] + sides(3)[2:], [SMEM] + [V...  3.68 us
    pallas_call x1, Pallas kernels, shards(): call(temporal_body, [(8, 48, 1024)], [VMEM, VMEM], TEMPORAL_FLOPS, 4 << 20)  3.28 us
  transfers between devices with their start and end apart: 14, of which 5 were waited for; matrix products, arithmetic and copies ran while one was open for 0% of the time, Pallas kernels for 7%

profile of v3, /device:TPU:65, one launch (start us, length us, event | category | flops | bytes accessed | tf_op | source)
XLA Modules:
  0.0 148.6 jit_solution(13905716150456749919)
XLA Ops:
  0.6 0.0 copy-start
  0.6 2.8 %split.1 = (bf16[8,64,1024]{2,1,0:T(8,128)(2,1)}, bf16[4,4,4,32,128]{4,3,2,1,0:T(8,128)(2,1)}, bf16[4,4,4,32,128]{4,3,2,1,0:T(8,128)(2,1)}) custom-call(bf16[128,1024]{1,0:T(8,128)(2,1)} %bitcast.9, bf16[128,1024]{1,0:T(8,128)(2,1)} %bitcast.10, bf16[128,1024]{1,0:T(8,128)(2,1)} %bitcast.11, bf16[128,1024]{1,0:T(8,128)(2,1)} %bitcast.12), custom_call_target="tpu_custom_call" | custom-call | flops 1048576 | bytes 3145728 | tf_op jit(solution)/shard_map/split/pallas_call | solution.py:373
  3.5 0.0 copy-start.4
  3.5 0.0 copy-start.1
  3.5 0.0 copy-start.2
  3.5 11.8 %all-to-all-start = ((bf16[8,64,1024]{2,1,0:T(8,128)(2,1)}), bf16[8,64,1024]{2,1,0:T(8,128)(2,1)S(1)}, u32[]{:S(2)}, u32[]{:S(2)}) async-start(bf16[8,64,1024]{2,1,0:T(8,128)(2,1)} %get-tuple-element.47), calls=%async_computation | async-start | bytes 2097152 | tf_op jit(solution)/shard_map/all_to_all | solution.py:358
  15.3 0.0 copy-done.4
  15.3 3.1 %collective-permute-start = (bf16[4,4,4,32,128]{4,3,2,1,0:T(8,128)(2,1)S(1)}, bf16[4,4,4,32,128]{4,3,2,1,0:T(8,128)(2,1)S(1)}, u32[]{:S(2)}, u32[]{:S(2)}) collective-permute-start(bf16[4,4,4,32,128]{4,3,2,1,0:T(8,128)(2,1)S(1)} %copy-done.4), channel_id=1, source_target_pairs={{0,8},{8,0},{16,24},{24,16},{32,40},{40,32},{48,56},{56,48},{64,72... | collective-permute-start | bytes 1572872 | tf_op jit(solution)/shard_map/ppermute | solution.py:355
  18.4 0.0 copy-done
  18.4 0.2 dynamic-slice_reduce_fusion
  18.6 0.1 pad_add_fusion.scal
  18.7 0.0 copy-start.3
  18.7 1.2 collective-permute-done.got
  19.9 0.0 copy-done.1
  19.9 0.0 copy-done.2
  19.9 0.0 copy-done.3
  19.9 1.7 %halo.1 = (bf16[4,4,8,32,128]{4,3,2,1,0:T(8,128)(2,1)S(1)}, bf16[4,9,32,128]{3,2,1,0:T(8,128)(2,1)}, bf16[4,9,32,128]{3,2,1,0:T(8,128)(2,1)}, bf16[4,5,32,128]{3...) custom-call(s32[4]{0:T(128)S(1)} %pad_add_fusion.scal, s32[8]{0:T(128)S(1)} %copy-done.3, ...), custom_call_target="tpu_custom_call" | custom-call | flops 268435456 | bytes 3145728 | tf_op jit(solution)/shard_map/halo/pallas_call | solution.py:380
  21.7 3.1 %collective-permute-start.1 = (bf16[4,4,32,128]{3,2,1,0:T(8,128)(2,1)S(1)}, bf16[4,4,32,128]{3,2,1,0:T(8,128)(2,1)S(1)}, u32[]{:S(2)}, u32[]{:S(2)}) collective-permute-start(bf16[4,4,32,128]{3,2,1,0:T(8,128)(2,1)S(1)} %get-tuple-element.33), channel_id=1, source_target_pairs={{0,16},{8,24},{48,32},{56,40},{64,80},{72,88},{112,96},{120,104},{... | collective-permute-start | bytes 393224 | tf_op jit(solution)/shard_map/ppermute | solution.py:336
  24.8 11.9 %collective-permute-start.4 = (bf16[4,5,32,128]{3,2,1,0:T(8,128)(2,1)}, bf16[4,5,32,128]{3,2,1,0:T(8,128)(2,1)S(1)}, u32[]{:S(2)}, u32[]{:S(2)}) collective-permute-start(bf16[4,5,32,128]{3,2,1,0:T(8,128)(2,1)} %get-tuple-element.36), channel_id=1, source_target_pairs={{0,496},{8,504},{48,64},{56,72},{64,48},{72,56},{112,128},{120,136... | collective-permute-start | bytes 491528 | tf_op jit(solution)/shard_map/ppermute | solution.py:336
  36.7 0.0 collective-permute-done.1
  36.7 1.3 collective-permute-start.5
  38.0 7.5 %collective-permute-start.2 = (bf16[4,9,32,128]{3,2,1,0:T(8,128)(2,1)}, bf16[4,9,32,128]{3,2,1,0:T(8,128)(2,1)S(1)}, u32[]{:S(2)}, u32[]{:S(2)}) collective-permute-start(bf16[4,9,32,128]{3,2,1,0:T(8,128)(2,1)} %get-tuple-element.34), channel_id=1, source_target_pairs={{0,16},{8,24},{16,32},{24,40},{32,48},{40,56},{64,80},{72,88},{80,... | collective-permute-start | bytes 884744 | tf_op jit(solution)/shard_map/ppermute | solution.py:336
  45.5 1.3 collective-permute-start.3
  46.8 22.2 %all-to-all-done.arrived = bf16[8,64,1024]{2,1,0:T(8,128)(2,1)S(1)} async-done(((bf16[8,64,1024]{2,1,0:T(8,128)(2,1)}), bf16[8,64,1024]{2,1,0:T(8,128)(2,1)S(1)}, u32[]{:S(2)}, u32[]{:S(2)}) %all-to-all-start) | async-done | bytes 1048608 | tf_op jit(solution)/shard_map/all_to_all | solution.py:358
  69.0 3.3 %temporal.1 = bf16[8,48,1024]{2,1,0:T(8,128)(2,1)} custom-call(bf16[8,64,1024]{2,1,0:T(8,128)(2,1)S(1)} %all-to-all-done.arrived, f32[8,1,1024]{2,1,0:T(1,128)S(1)} %get-tuple-element.49.gates), custom_call_target="tpu_custom_call" | custom-call | flops 34359738368 | bytes 4194304 | tf_op jit(solution)/shard_map/temporal/pallas_call | solution.py:391
  72.3 16.0 %all-to-all-start.1 = ((bf16[8,48,1024]{2,1,0:T(8,128)(2,1)}), bf16[8,48,1024]{2,1,0:T(8,128)(2,1)S(1)}, u32[]{:S(2)}, u32[]{:S(2)}) async-start(bf16[8,48,1024]{2,1,0:T(8,128)(2,1)} %temporal.1), calls=%async_computation.1 | async-start | bytes 1572864 | tf_op jit(solution)/shard_map/all_to_all | solution.py:358
  88.3 0.0 collective-permute-done.4.in_a
  88.3 0.0 collective-permute-done.5.in_b
  88.3 0.0 collective-permute-done.2.from_left
  88.3 0.0 collective-permute-done.3.from_right
  88.3 3.7 %spatial.1 = (bf16[3,4,8,32,128]{4,3,2,1,0:T(8,128)(2,1)S(1)}, bf16[3,5,32,128]{3,2,1,0:T(8,128)(2,1)S(1)}, bf16[3,4,32,128]{3,2,1,0:T(8,128)(2,1)S(1)}) custom-call(s32[4]{0:T(128)S(1)} %pad_add_fusion.scal, bf16[4,4,8,32,128]{4,3,2,1,0:T(8,128)(2,1)S(1)} %get-tuple-element.30.whole, bf16[4,9,32,128]{3,2,1,0:T(8,128)(2,1)S(1)} %collective-permute-done.2.from_left, ...), custom_call_target="tpu_custom_call" | custom-call | flops 53687091200 | bytes 4194304 | tf_op jit(solution)/shard_map/spatial/pallas_call | solution.py:396
  92.0 1.3 collective-permute-start.8
  93.3 0.7 sides.1
  94.0 1.3 collective-permute-start.6
  95.3 1.3 collective-permute-start.7
  96.6 0.0 collective-permute-done.8
  96.6 15.3 %collective-permute-start.9 = (bf16[3,5,32,128]{3,2,1,0:T(8,128)(2,1)S(1)}, bf16[3,5,32,128]{3,2,1,0:T(8,128)(2,1)S(1)}, u32[]{:S(2)}, u32[]{:S(2)}) collective-permute-start(bf16[3,5,32,128]{3,2,1,0:T(8,128)(2,1)S(1)} %get-tuple-element.43), channel_id=1, source_target_pairs={{0,496},{8,504},{48,64},{56,72},{64,48},{72,56},{112,128},{120,136... | collective-permute-start | bytes 368648 | tf_op jit(solution)/shard_map/ppermute | solution.py:336
  111.9 1.3 collective-permute-start.10
  113.2 20.4 %collective-permute-done.10.in_b = bf16[3,4,32,128]{3,2,1,0:T(8,128)(2,1)S(1)} collective-permute-done((bf16[3,4,32,128]{3,2,1,0:T(8,128)(2,1)S(1)}, bf16[3,4,32,128]{3,2,1,0:T(8,128)(2,1)S(1)}, u32[]{:S(2)}, u32[]{:S(2)}) %collective-permute-start.10) | collective-permute-done | bytes 98336 | tf_op jit(solution)/shard_map/ppermute | solution.py:336
  133.6 8.3 %collective-permute-done.9.in_a = bf16[3,5,32,128]{3,2,1,0:T(8,128)(2,1)S(1)} collective-permute-done((bf16[3,5,32,128]{3,2,1,0:T(8,128)(2,1)S(1)}, bf16[3,5,32,128]{3,2,1,0:T(8,128)(2,1)S(1)}, u32[]{:S(2)}, u32[]{:S(2)}) %collective-permute-start.9) | collective-permute-done | bytes 122912 | tf_op jit(solution)/shard_map/ppermute | solution.py:336
  141.8 0.0 collective-permute-done.6.from_left
  141.8 0.0 collective-permute-done.7.from_right
  141.8 1.4 gather.1
  143.2 2.5 %collective-permute-start.11 = (bf16[3,4,4,32,128]{4,3,2,1,0:T(8,128)(2,1)S(1)}, bf16[3,4,4,32,128]{4,3,2,1,0:T(8,128)(2,1)S(1)}, u32[]{:S(2)}, u32[]{:S(2)}) collective-permute-start(bf16[3,4,4,32,128]{4,3,2,1,0:T(8,128)(2,1)S(1)} %get-tuple-element.46), channel_id=1, source_target_pairs={{0,8},{8,0},{16,24},{24,16},{32,40},{40,32},{48,56},{56,48},{64,72... | collective-permute-start | bytes 1179656 | tf_op jit(solution)/shard_map/ppermute | solution.py:355
  145.7 1.3 collective-permute-done.11.got
  147.0 0.0 all-to-all-done.1.times
  147.0 1.7 %final.1 = (bf16[128,1024]{1,0:T(8,128)(2,1)}, bf16[128,1024]{1,0:T(8,128)(2,1)}, bf16[128,1024]{1,0:T(8,128)(2,1)}) custom-call(s32[4]{0:T(128)S(1)} %pad_add_fusion.scal, bf16[3,4,4,32,128]{4,3,2,1,0:T(8,128)(2,1)S(1)} %get-tuple-element.45.keep, bf16[3,4,4,32,128]{4,3,2,1,0:T(8,128)(2,1)S(1)} %collective-permute-done.11.got, ...), custom_call_target="tpu_custom_call" | custom-call | flops 1048576 | bytes 3145728 | tf_op jit(solution)/shard_map/final/pallas_call | solution.py:412
Async XLA Ops:
  0.6 17.8 %copy-start = (s32[8,2]{0,1:T(2,128)S(1)}, s32[8,2]{0,1:T(2,128)}, u32[]{:S(2)}) copy-start(s32[8,2]{0,1:T(2,128)} %param.11) | copy-start | bytes 196
  3.5 11.8 %copy-start.4 = (bf16[4,4,4,32,128]{4,3,2,1,0:T(8,128)(2,1)S(1)}, bf16[4,4,4,32,128]{4,3,2,1,0:T(8,128)(2,1)}, u32[]{:S(2)}) copy-start(bf16[4,4,4,32,128]{4,3,2,1,0:T(8,128)(2,1)} %get-tuple-element.29) | copy-start | bytes 1572868
  3.5 16.4 %copy-start.1 = (bf16[4,4,4,32,128]{4,3,2,1,0:T(8,128)(2,1)S(1)}, bf16[4,4,4,32,128]{4,3,2,1,0:T(8,128)(2,1)}, u32[]{:S(2)}) copy-start(bf16[4,4,4,32,128]{4,3,2,1,0:T(8,128)(2,1)} %get-tuple-element.28.own) | copy-start | bytes 1572868
  3.5 16.4 %copy-start.2 = (f32[64,1024]{1,0:T(8,128)S(1)}, f32[64,1024]{1,0:T(8,128)}, u32[]{:S(2)}) copy-start(f32[64,1024]{1,0:T(8,128)} %table.1) | copy-start | bytes 786436
  3.5 65.5 %all-to-all-start = ((bf16[8,64,1024]{2,1,0:T(8,128)(2,1)}), bf16[8,64,1024]{2,1,0:T(8,128)(2,1)S(1)}, u32[]{:S(2)}, u32[]{:S(2)}) async-start(bf16[8,64,1024]{2,1,0:T(8,128)(2,1)} %get-tuple-element.47), calls=%async_computation | async-start | bytes 2097152 | tf_op jit(solution)/shard_map/all_to_all | solution.py:358
  15.3 4.7 %collective-permute-start = (bf16[4,4,4,32,128]{4,3,2,1,0:T(8,128)(2,1)S(1)}, bf16[4,4,4,32,128]{4,3,2,1,0:T(8,128)(2,1)S(1)}, u32[]{:S(2)}, u32[]{:S(2)}) collective-permute-start(bf16[4,4,4,32,128]{4,3,2,1,0:T(8,128)(2,1)S(1)} %copy-done.4), channel_id=1, source_target_pairs={{0,8},{8,0},{16,24},{24,16},{32,40},{40,32},{48,56},{56,48},{64,72... | collective-permute-start | bytes 1572872 | tf_op jit(solution)/shard_map/ppermute | solution.py:355
  18.7 1.2 copy-start.3
  21.7 15.0 %collective-permute-start.1 = (bf16[4,4,32,128]{3,2,1,0:T(8,128)(2,1)S(1)}, bf16[4,4,32,128]{3,2,1,0:T(8,128)(2,1)S(1)}, u32[]{:S(2)}, u32[]{:S(2)}) collective-permute-start(bf16[4,4,32,128]{3,2,1,0:T(8,128)(2,1)S(1)} %get-tuple-element.33), channel_id=1, source_target_pairs={{0,16},{8,24},{48,32},{56,40},{64,80},{72,88},{112,96},{120,104},{... | collective-permute-start | bytes 393224 | tf_op jit(solution)/shard_map/ppermute | solution.py:336
  24.8 63.5 %collective-permute-start.4 = (bf16[4,5,32,128]{3,2,1,0:T(8,128)(2,1)}, bf16[4,5,32,128]{3,2,1,0:T(8,128)(2,1)S(1)}, u32[]{:S(2)}, u32[]{:S(2)}) collective-permute-start(bf16[4,5,32,128]{3,2,1,0:T(8,128)(2,1)} %get-tuple-element.36), channel_id=1, source_target_pairs={{0,496},{8,504},{48,64},{56,72},{64,48},{72,56},{112,128},{120,136... | collective-permute-start | bytes 491528 | tf_op jit(solution)/shard_map/ppermute | solution.py:336
  36.7 51.6 %collective-permute-start.5 = (bf16[4,4,32,128]{3,2,1,0:T(8,128)(2,1)S(1)}, bf16[4,4,32,128]{3,2,1,0:T(8,128)(2,1)S(1)}, u32[]{:S(2)}, u32[]{:S(2)}) collective-permute-start(bf16[4,4,32,128]{3,2,1,0:T(8,128)(2,1)S(1)} %collective-permute-done.1), channel_id=1, source_target_pairs={{16,496},{24,504},{32,64},{40,72},{80,48},{88,56},{96,128},{104,13... | collective-permute-start | bytes 393224 | tf_op jit(solution)/shard_map/ppermute | solution.py:336
  38.0 50.3 %collective-permute-start.2 = (bf16[4,9,32,128]{3,2,1,0:T(8,128)(2,1)}, bf16[4,9,32,128]{3,2,1,0:T(8,128)(2,1)S(1)}, u32[]{:S(2)}, u32[]{:S(2)}) collective-permute-start(bf16[4,9,32,128]{3,2,1,0:T(8,128)(2,1)} %get-tuple-element.34), channel_id=1, source_target_pairs={{0,16},{8,24},{16,32},{24,40},{32,48},{40,56},{64,80},{72,88},{80,... | collective-permute-start | bytes 884744 | tf_op jit(solution)/shard_map/ppermute | solution.py:336
  45.5 42.8 %collective-permute-start.3 = (bf16[4,9,32,128]{3,2,1,0:T(8,128)(2,1)}, bf16[4,9,32,128]{3,2,1,0:T(8,128)(2,1)S(1)}, u32[]{:S(2)}, u32[]{:S(2)}) collective-permute-start(bf16[4,9,32,128]{3,2,1,0:T(8,128)(2,1)} %get-tuple-element.35), channel_id=1, source_target_pairs={{16,0},{24,8},{32,16},{40,24},{48,32},{56,40},{80,64},{88,72},{96,... | collective-permute-start | bytes 884744 | tf_op jit(solution)/shard_map/ppermute | solution.py:336
  72.3 74.7 %all-to-all-start.1 = ((bf16[8,48,1024]{2,1,0:T(8,128)(2,1)}), bf16[8,48,1024]{2,1,0:T(8,128)(2,1)S(1)}, u32[]{:S(2)}, u32[]{:S(2)}) async-start(bf16[8,48,1024]{2,1,0:T(8,128)(2,1)} %temporal.1), calls=%async_computation.1 | async-start | bytes 1572864 | tf_op jit(solution)/shard_map/all_to_all | solution.py:358
  92.0 4.6 %collective-permute-start.8 = (bf16[3,4,32,128]{3,2,1,0:T(8,128)(2,1)S(1)}, bf16[3,4,32,128]{3,2,1,0:T(8,128)(2,1)S(1)}, u32[]{:S(2)}, u32[]{:S(2)}) collective-permute-start(bf16[3,4,32,128]{3,2,1,0:T(8,128)(2,1)S(1)} %get-tuple-element.42), channel_id=1, source_target_pairs={{0,16},{8,24},{48,32},{56,40},{64,80},{72,88},{112,96},{120,104},{... | collective-permute-start | bytes 294920 | tf_op jit(solution)/shard_map/ppermute | solution.py:336
  94.0 47.9 %collective-permute-start.6 = (bf16[3,9,32,128]{3,2,1,0:T(8,128)(2,1)S(1)}, bf16[3,9,32,128]{3,2,1,0:T(8,128)(2,1)S(1)}, u32[]{:S(2)}, u32[]{:S(2)}) collective-permute-start(bf16[3,9,32,128]{3,2,1,0:T(8,128)(2,1)S(1)} %get-tuple-element.39), channel_id=1, source_target_pairs={{0,16},{8,24},{16,32},{24,40},{32,48},{40,56},{64,80},{72,88},{80,... | collective-permute-start | bytes 663560 | tf_op jit(solution)/shard_map/ppermute | solution.py:336
  95.3 46.6 %collective-permute-start.7 = (bf16[3,9,32,128]{3,2,1,0:T(8,128)(2,1)S(1)}, bf16[3,9,32,128]{3,2,1,0:T(8,128)(2,1)S(1)}, u32[]{:S(2)}, u32[]{:S(2)}) collective-permute-start(bf16[3,9,32,128]{3,2,1,0:T(8,128)(2,1)S(1)} %get-tuple-element.40), channel_id=1, source_target_pairs={{16,0},{24,8},{32,16},{40,24},{48,32},{56,40},{80,64},{88,72},{96,... | collective-permute-start | bytes 663560 | tf_op jit(solution)/shard_map/ppermute | solution.py:336
  96.6 45.2 %collective-permute-start.9 = (bf16[3,5,32,128]{3,2,1,0:T(8,128)(2,1)S(1)}, bf16[3,5,32,128]{3,2,1,0:T(8,128)(2,1)S(1)}, u32[]{:S(2)}, u32[]{:S(2)}) collective-permute-start(bf16[3,5,32,128]{3,2,1,0:T(8,128)(2,1)S(1)} %get-tuple-element.43), channel_id=1, source_target_pairs={{0,496},{8,504},{48,64},{56,72},{64,48},{72,56},{112,128},{120,136... | collective-permute-start | bytes 368648 | tf_op jit(solution)/shard_map/ppermute | solution.py:336
  111.9 21.7 %collective-permute-start.10 = (bf16[3,4,32,128]{3,2,1,0:T(8,128)(2,1)S(1)}, bf16[3,4,32,128]{3,2,1,0:T(8,128)(2,1)S(1)}, u32[]{:S(2)}, u32[]{:S(2)}) collective-permute-start(bf16[3,4,32,128]{3,2,1,0:T(8,128)(2,1)S(1)} %collective-permute-done.8), channel_id=1, source_target_pairs={{16,496},{24,504},{32,64},{40,72},{80,48},{88,56},{96,128},{104,13... | collective-permute-start | bytes 294920 | tf_op jit(solution)/shard_map/ppermute | solution.py:336
  143.2 3.8 %collective-permute-start.11 = (bf16[3,4,4,32,128]{4,3,2,1,0:T(8,128)(2,1)S(1)}, bf16[3,4,4,32,128]{4,3,2,1,0:T(8,128)(2,1)S(1)}, u32[]{:S(2)}, u32[]{:S(2)}) collective-permute-start(bf16[3,4,4,32,128]{4,3,2,1,0:T(8,128)(2,1)S(1)} %get-tuple-element.46), channel_id=1, source_target_pairs={{0,8},{8,0},{16,24},{24,16},{32,40},{40,32},{48,56},{56,48},{64,72... | collective-permute-start | bytes 1179656 | tf_op jit(solution)/shard_map/ppermute | solution.py:355
